TPU v7x, 32 devices: a whole 2x2x4 slice. The times are simulated.
32 devices in a mesh: dp: 4 (over z), row: 4 (over y, x), col: 2 (over core).
Axes of the slice: x: 2, y: 2, z: 4, core: 2. Of those that a mesh axis runs over, the one named last changes fastest.
Arguments:
- layer_in: bfloat16 [8192, 768], P(('dp', 'row')), may hold values from -6 to 6
- w_qkv: bfloat16 [3, 768, 768], P(None, 'col', 'row'), may hold values from -0.21875 to 0.21875
- w_proj: bfloat16 [768, 768], P('row', 'col'), may hold values from -3.5 to 3.5
- rel_bias: float32 [12, 32], replicated, may hold values from -4 to 4
- rel_bucket: int32 [2047], replicated, may hold values from 0 to 31
- segment_ids: int32 [8, 1024], P(('dp', 'col')), may hold values from 0 to 2, never falling along the last dimension, each value on 1 to 512 neighbouring positions
- gain_attn: float32 [768], replicated, may hold values from 0.1 to 1.9
- gain_ffn: float32 [768], replicated, may hold values from 0.1 to 1.9
- w_router: float32 [768, 16], replicated, may hold values from -0.109375 to 0.109375
- routes: int32 [8192, 1], P(('dp', 'row')), may hold values from 0 to 15; in each aligned block of 512 rows (0 to 511, 512 to 1023, ...) at most 64 rows name the same one
- w_up: bfloat16 [16, 3072, 768], P(('row', 'col')), may hold values from -0.21875 to 0.21875
- w_down: bfloat16 [16, 3072, 768], P(('row', 'col')), may hold values from -2.5 to 2.5
- d_layer: bfloat16 [8192, 768], P(('dp', 'row'), 'col'), may hold values from -6 to 6
Outputs:
- layer_out: float32 [8192, 768], P(('dp', 'row'), 'col')
- d_layer_in: float32 [8192, 768], P(('dp', 'row'), 'col')
- d_w_qkv: float32 [3, 768, 768], P(None, 'col', 'row')
- d_w_proj: float32 [768, 768], P('row', 'col')
- d_rel_bias: float32 [12, 32], replicated
- d_gain_attn: float32 [768], replicated
- d_gain_ffn: float32 [768], replicated
- d_w_router: float32 [768, 16], replicated
- d_w_up: float32 [16, 3072, 768], P(('row', 'col'), 'dp')
- d_w_down: float32 [16, 3072, 768], P(('row', 'col'), 'dp')
Inputs may be any that keep to these rules, and one draw needn't show every extreme that they name: `routes`: in each aligned block of 512 rows (the rows of one device) no expert is named by more than 64 rows. `segment_ids`: within each sequence the ids never fall; a document has 1 to 512 tokens.
All inputs are finite; a program needn't handle non-finite values.
Results may differ from a plain program's by a relative error of at most 0.017.
Values may be sent and summed in bfloat16 or wider, within the bound.
No kernel may reach another device: no remote copies, remote signals or barrier semaphores. Data moves between devices by JAX's collectives and lax.ppermute only.
A program may use at most 192 MiB of HBM per device.

v0:
```python
from functools import partial

import jax
import jax.numpy as jnp
from jax import lax
from jax.sharding import PartitionSpec as P

H = 12
HD = 64
NB = 32
EXP_DEV = 2


epsilon = 1e-06
highest = lax.Precision.HIGHEST


def skewed_bias(table_seg, block_rows, length):
    heads_dev, seg_len = table_seg.shape
    tiled = jnp.tile(table_seg, (1, block_rows + 1))[:, : block_rows * (seg_len + 1)]
    shifted = tiled.reshape(heads_dev, block_rows, seg_len + 1)[:, :, :length]
    return jnp.flip(shifted, axis=1)


def block_scores(queries, keys_all, segments, bias_table, begin_at, block_rows):
    length = keys_all.shape[0]
    query_rows = lax.dynamic_slice_in_dim(queries, begin_at, block_rows, 0)
    seg_rows = lax.dynamic_slice_in_dim(segments, begin_at, block_rows, 0)
    raw_scores = jnp.einsum(
        "qhd,khd->hqk", query_rows, keys_all, preferred_element_type=jnp.float32
    )
    seg_start = length - begin_at - block_rows
    table_seg = lax.dynamic_slice_in_dim(bias_table, seg_start, length + block_rows - 1, 1)
    scores = raw_scores * queries.shape[2] ** (-0.5) + skewed_bias(table_seg, block_rows, length)
    same_doc = seg_rows[:, None] == segments[None, :]
    return (jnp.where(same_doc[None], scores, -1000000000.0), query_rows, seg_start, table_seg)


def attend_forward(queries, keys_all, values_all, segments, bias_table, block_rows):
    length = queries.shape[0]
    starts = jnp.arange(length // block_rows, dtype=jnp.int32) * block_rows

    def one_block(begin_at):
        scores, query_rows, seg_start, table_seg = block_scores(
            queries, keys_all, segments, bias_table, begin_at, block_rows
        )
        row_max = jnp.max(scores, axis=-1, keepdims=True)
        weights = jnp.exp(scores - row_max)
        totals = jnp.sum(weights, axis=-1, keepdims=True)
        attn_probs = (weights / totals).astype(jnp.bfloat16)
        head_rows = jnp.einsum(
            "hqk,khd->qhd", attn_probs, values_all, preferred_element_type=jnp.float32
        )
        return (head_rows, (row_max + jnp.log(totals))[..., 0])

    head_out, log_total = lax.map(one_block, starts)
    return (head_out.reshape(length, -1), log_total)


def attend_backward(
    queries, keys_all, values_all, segments, bias_table, block_rows, log_total, d_head
):
    length, heads_dev, head_size = queries.shape
    starts = jnp.arange(length // block_rows, dtype=jnp.int32) * block_rows
    d_head = d_head.reshape(length, heads_dev, head_size)

    def one_block(carry, packed):
        d_keys, d_values, d_table = carry
        begin_at, total_rows = packed
        scores, query_rows, seg_start, table_seg = block_scores(
            queries, keys_all, segments, bias_table, begin_at, block_rows
        )
        attn_probs = jnp.exp(scores - total_rows[:, :, None])
        grad_rows = lax.dynamic_slice_in_dim(d_head, begin_at, block_rows, 0)
        d_values = d_values + jnp.einsum(
            "hqk,qhd->khd",
            attn_probs.astype(jnp.bfloat16),
            grad_rows,
            preferred_element_type=jnp.float32,
        )
        d_probs = jnp.einsum(
            "qhd,khd->hqk", grad_rows, values_all, preferred_element_type=jnp.float32
        )
        d_scores = attn_probs * (d_probs - jnp.sum(attn_probs * d_probs, axis=-1, keepdims=True))
        skew_value, skew_pull = jax.vjp(
            lambda seg_part: skewed_bias(seg_part, block_rows, length), table_seg
        )
        d_seg = skew_pull(d_scores)[0]
        seg_len = table_seg.shape[1]
        current = lax.dynamic_slice_in_dim(d_table, seg_start, seg_len, 1)
        d_table = lax.dynamic_update_slice_in_dim(d_table, current + d_seg, seg_start, 1)
        d_raw = (d_scores * head_size ** (-0.5)).astype(jnp.bfloat16)
        d_query = jnp.einsum("hqk,khd->qhd", d_raw, keys_all, preferred_element_type=jnp.float32)
        d_keys = d_keys + jnp.einsum(
            "hqk,qhd->khd", d_raw, query_rows, preferred_element_type=jnp.float32
        )
        return ((d_keys, d_values, d_table), d_query)

    zero_keys = jnp.zeros((length, heads_dev, head_size), jnp.float32)
    zero_table = jnp.zeros((heads_dev, 2 * length - 1), jnp.float32)
    carried, d_query = lax.scan(one_block, (zero_keys, zero_keys, zero_table), (starts, log_total))
    return (d_query.reshape(length, heads_dev, head_size), carried[0], carried[1], carried[2])


def to_experts(buffer, row_count, col_count, slot_count, half_width):
    shaped = buffer.reshape(row_count, col_count, EXP_DEV, slot_count, half_width)
    return shaped.transpose(2, 0, 3, 1, 4).reshape(
        EXP_DEV, row_count * slot_count, col_count * half_width
    )


def from_experts(tensor, row_count, col_count, slot_count, half_width):
    shaped = tensor.reshape(EXP_DEV, row_count, slot_count, col_count, half_width)
    return shaped.transpose(1, 3, 0, 2, 4).reshape(
        row_count * col_count, EXP_DEV, slot_count, half_width
    )


def shards(
    layer_in,
    w_qkv,
    w_proj,
    rel_bias,
    rel_bucket,
    segment_ids,
    gain_attn,
    gain_ffn,
    w_router,
    routes,
    w_up,
    w_down,
    d_layer,
):
    row_count = lax.axis_size("row")
    col_count = lax.axis_size("col")
    row_at = lax.axis_index("row")
    col_at = lax.axis_index("col")
    tok_dev, width = layer_in.shape
    slot_count = max(2, tok_dev // 8)
    half_width = width // col_count
    length = segment_ids.shape[1]
    heads_dev = w_qkv.shape[2] // HD
    experts_all = EXP_DEV * row_count * col_count
    block_rows = min(512, length)
    input_full = layer_in.astype(jnp.float32)
    scale_attn = lax.rsqrt(jnp.mean(input_full * input_full, axis=-1, keepdims=True) + epsilon)
    normed = (input_full * scale_attn * gain_attn).astype(jnp.bfloat16)
    input_half = lax.dynamic_slice_in_dim(input_full, col_at * half_width, half_width, 1)
    gain_half = lax.dynamic_slice_in_dim(gain_attn, col_at * half_width, half_width, 0)
    normed_half = lax.dynamic_slice_in_dim(normed, col_at * half_width, half_width, 1)
    gathered = lax.all_gather(normed_half, "row", axis=0, tiled=True)
    part_rows = gathered
    qkv_sum = lax.psum_scatter(
        jnp.einsum("td,kde->tke", part_rows, w_qkv, preferred_element_type=jnp.float32),
        "col",
        scatter_dimension=0,
        tiled=True,
    )
    qkv_low = qkv_sum.astype(jnp.bfloat16).reshape(length, 3, heads_dev, HD)
    queries = qkv_low[:, 0]
    keys_all = qkv_low[:, 1]
    values_all = qkv_low[:, 2]
    segments = segment_ids[0]
    buckets = (rel_bucket[:, None] == jnp.arange(NB, dtype=jnp.int32)[None, :]).astype(jnp.float32)
    bias_rows = lax.dynamic_slice_in_dim(rel_bias, row_at * heads_dev, heads_dev, 0)
    bias_table = jnp.einsum("hb,ob->ho", bias_rows, buckets, precision=highest)
    head_out, log_total = attend_forward(
        queries, keys_all, values_all, segments, bias_table, block_rows
    )
    heads_all = lax.all_gather(head_out.astype(jnp.bfloat16), "col", axis=0, tiled=True)
    part_rows = heads_all
    attn_out = lax.psum_scatter(
        jnp.dot(part_rows, w_proj, preferred_element_type=jnp.float32),
        "row",
        scatter_dimension=0,
        tiled=True,
    )
    middle = input_half + attn_out
    routed = routes[:, 0]
    chosen = routed[:, None] == jnp.arange(experts_all, dtype=jnp.int32)[None, :]
    counts = jnp.cumsum(chosen.astype(jnp.int32), axis=0)
    slot_index = jnp.sum(jnp.where(chosen, counts, 0), axis=-1) - 1
    placed = routed * slot_count + slot_index
    grads_in = d_layer.astype(jnp.float32)
    empty = jnp.zeros((experts_all * slot_count, half_width), jnp.float32)
    send_shape = (row_count * col_count, EXP_DEV, slot_count, half_width)
    send_mid = empty.at[placed].set(middle).reshape(send_shape)
    send_grad = empty.at[placed].set(grads_in).reshape(send_shape)
    got_mid, got_grad = (
        lax.all_to_all(send_mid, ("row", "col"), split_axis=0, concat_axis=0, tiled=True),
        lax.all_to_all(send_grad, ("row", "col"), split_axis=0, concat_axis=0, tiled=True),
    )
    token_rows = to_experts(got_mid, row_count, col_count, slot_count, half_width)
    token_grads = to_experts(got_grad, row_count, col_count, slot_count, half_width)
    local_ids = (row_at * col_count + col_at) * EXP_DEV + jnp.arange(EXP_DEV, dtype=jnp.int32)
    picked = (local_ids[:, None] == jnp.arange(experts_all, dtype=jnp.int32)[None, :])[:, None, :]
    scale_ffn = lax.rsqrt(jnp.mean(token_rows * token_rows, axis=-1, keepdims=True) + epsilon)
    hidden = token_rows * scale_ffn * gain_ffn
    gate_probs = jax.nn.softmax(
        jnp.einsum("esd,dn->esn", hidden, w_router, precision=highest), axis=-1
    )
    gating = jnp.sum(jnp.where(picked, gate_probs, 0.0), axis=-1)
    expert_in = hidden.astype(jnp.bfloat16)
    pre_act = jnp.einsum("esd,efd->esf", expert_in, w_up, preferred_element_type=jnp.float32)
    gelu_value, gelu_pull = jax.vjp(partial(jax.nn.gelu, approximate=True), pre_act)
    activated = gelu_value.astype(jnp.bfloat16)
    expert_out = jnp.einsum("esf,efd->esd", activated, w_down, preferred_element_type=jnp.float32)
    gated_out = gating[..., None] * expert_out
    d_expert = (gating[..., None] * token_grads).astype(jnp.bfloat16)
    d_gating = jnp.sum(token_grads * expert_out, axis=-1)
    d_down = jnp.einsum("esf,esd->efd", activated, d_expert, preferred_element_type=jnp.float32)
    d_activated = jnp.einsum("esd,efd->esf", d_expert, w_down, preferred_element_type=jnp.float32)
    d_pre = gelu_pull(d_activated)[0].astype(jnp.bfloat16)
    d_up = jnp.einsum("esf,esd->efd", d_pre, expert_in, preferred_element_type=jnp.float32)
    d_logits = d_gating[..., None] * gate_probs * (picked.astype(jnp.float32) - gating[..., None])
    d_hidden = jnp.einsum("esf,efd->esd", d_pre, w_up, preferred_element_type=jnp.float32)
    d_hidden = d_hidden + jnp.einsum("esn,dn->esd", d_logits, w_router, precision=highest)
    d_router = jnp.einsum("esd,esn->dn", hidden, d_logits, precision=highest)
    d_gain_ffn = jnp.sum(token_rows * scale_ffn * d_hidden, axis=(0, 1))
    scaled_ffn = d_hidden * gain_ffn
    d_rows = scale_ffn * scaled_ffn - token_rows * scale_ffn**3 * jnp.mean(
        scaled_ffn * token_rows, axis=-1, keepdims=True
    )
    back_out, back_grad = (
        lax.all_to_all(
            from_experts(gated_out, row_count, col_count, slot_count, half_width).astype(
                jnp.bfloat16
            ),
            ("row", "col"),
            split_axis=0,
            concat_axis=0,
            tiled=True,
        ).astype(jnp.float32),
        lax.all_to_all(
            from_experts(d_rows, row_count, col_count, slot_count, half_width).astype(jnp.bfloat16),
            ("row", "col"),
            split_axis=0,
            concat_axis=0,
            tiled=True,
        ).astype(jnp.float32),
    )
    layer_out = middle + back_out.reshape(experts_all * slot_count, half_width)[placed]
    d_middle = grads_in + back_grad.reshape(experts_all * slot_count, half_width)[placed]
    d_attn = d_middle.astype(jnp.bfloat16)
    grads_all = lax.all_gather(d_attn, "row", axis=0, tiled=True)
    d_w_proj = jnp.einsum("th,tk->hk", heads_all, grads_all, preferred_element_type=jnp.float32)
    part_rows = grads_all
    d_head = lax.psum_scatter(
        jnp.einsum("tk,hk->th", part_rows, w_proj, preferred_element_type=jnp.float32),
        "col",
        scatter_dimension=0,
        tiled=True,
    ).astype(jnp.bfloat16)
    d_queries, d_keys, d_values, d_table = attend_backward(
        queries, keys_all, values_all, segments, bias_table, block_rows, log_total, d_head
    )
    d_qkv = (
        jnp.stack([d_queries, d_keys, d_values], axis=1)
        .astype(jnp.bfloat16)
        .reshape(length, 3, heads_dev * HD)
    )
    d_qkv_all = lax.all_gather(d_qkv, "col", axis=0, tiled=True)
    d_w_qkv = jnp.einsum("td,tke->kde", gathered, d_qkv_all, preferred_element_type=jnp.float32)
    part_rows = d_qkv_all
    d_normed = lax.psum_scatter(
        jnp.einsum("tke,kde->td", part_rows, w_qkv, preferred_element_type=jnp.float32).astype(
            jnp.bfloat16
        ),
        "row",
        scatter_dimension=0,
        tiled=True,
    ).astype(jnp.float32)
    scaled_attn = d_normed * gain_half
    inner_sum = lax.psum(jnp.sum(scaled_attn * input_half, axis=-1), "col")
    d_layer_in = (
        d_middle
        + scale_attn * scaled_attn
        - input_half * scale_attn**3 * (inner_sum / width)[:, None]
    )
    d_gain_part = jnp.sum(input_half * scale_attn * d_normed, axis=0)
    d_rel_part = jnp.einsum("ho,ob->hb", d_table, buckets, precision=highest)
    d_w_qkv, d_w_proj = (
        lax.psum(d_w_qkv.astype(jnp.bfloat16), "dp").astype(jnp.float32),
        lax.psum(d_w_proj.astype(jnp.bfloat16), "dp").astype(jnp.float32),
    )
    gain_whole = lax.dynamic_update_slice_in_dim(
        jnp.zeros((width,), jnp.float32), d_gain_part, col_at * half_width, 0
    )
    rel_whole = lax.dynamic_update_slice_in_dim(
        jnp.zeros((H, NB), jnp.float32), d_rel_part, row_at * heads_dev, 0
    )
    d_gain_attn, d_gain_ffn, d_router, d_rel_bias = lax.psum(
        (gain_whole, d_gain_ffn, d_router, rel_whole), ("dp", "row", "col")
    )
    d_up, d_down = (
        lax.psum_scatter(d_up.astype(jnp.bfloat16), "dp", scatter_dimension=1, tiled=True).astype(
            jnp.float32
        ),
        lax.psum_scatter(d_down.astype(jnp.bfloat16), "dp", scatter_dimension=1, tiled=True).astype(
            jnp.float32
        ),
    )
    return (
        layer_out,
        d_layer_in,
        d_w_qkv,
        d_w_proj,
        d_rel_bias,
        d_gain_attn,
        d_gain_ffn,
        d_router,
        d_up,
        d_down,
    )


def solution(mesh):
    placed = (
        P(("dp", "row"), None),
        P(None, "col", "row"),
        P("row", "col"),
        P(),
        P(),
        P(("dp", "col"), None),
        P(),
        P(),
        P(),
        P(("dp", "row"), None),
        P(("row", "col"), None, None),
        P(("row", "col"), None, None),
        P(("dp", "row"), "col"),
    )
    return jax.shard_map(
        shards,
        mesh=mesh,
        in_specs=placed,
        out_specs=(
            P(("dp", "row"), "col"),
            P(("dp", "row"), "col"),
            P(None, "col", "row"),
            P("row", "col"),
            P(),
            P(),
            P(),
            P(),
            P(("row", "col"), "dp", None),
            P(("row", "col"), "dp", None),
        ),
        check_vma=False,
    )
```

profile of v0, /device:TPU:0, one launch (start us, length us, event | category | flops | bytes accessed | tf_op | source)
XLA Modules:
  0.0 1446.9 jit_solution(7449763448028767605)
XLA Ops:
  12.2 33.8 %all-gather.4.cloned.1.call-done = bf16[2048,384]{1,0:T(8,128)(2,1)} async-done(((bf16[512,384]{1,0:T(8,128)(2,1)}), bf16[2048,384]{1,0:T(8,128)(2,1)}) %all-gather.4.cloned.1.call-update) | async-done | bytes 1572880 | tf_op jit(solution)/shard_map/all_gather | solution.py:151
  46.0 5.0 fusion.93
  53.1 10.7 reduce-scatter.7.cloned.1.call-done
  67.5 244.6 %while.37 = (s32[]{:T(128)}, bf16[2,512,3,64]{1,3,2,0:T(8,128)(2,1)}, f32[2,3,512]{2,1,0:T(4,128)}, s32[2]{0:T(128)S(1)}, s32[1024]{0:T(1024)S(1)}, /*index=5*/s...) while((s32[]{:T(128)}, ...), condition=%wide.region_5.6_spmd, body=%wide.region_2.5_spmd.sunk | while | flops 417331712 | bytes 163666352 | solution.py:56
  87.2 4.9 tile.36
  92.1 15.2 %reshape.415 = f32[2362365]{0:T(1024)} reshape(f32[3,513,1535]{2,1,0:T(8,128)} %tile.36) | data formatting | bytes 18898920 | tf_op jit(solution)/shard_map/while
  107.3 13.8 tile.37
  125.7 6.5 copy.84
  132.3 6.7 slice.79
  139.0 48.6 %rev.34 = f32[3,512,1024]{2,1,0:T(8,128)} reverse(f32[3,512,1024]{2,1,0:T(8,128)} %slice.79), dimensions={1} | reverse | bytes 12582912 | tf_op jit(solution)/shard_map/while/body/eval_jaxpr/jit(_flip)/rev | solution.py:22
  187.6 4.6 fusion.139
  202.0 4.9 tile.36
  206.9 15.2 %reshape.415 = f32[2362365]{0:T(1024)} reshape(f32[3,513,1535]{2,1,0:T(8,128)} %tile.36) | data formatting | bytes 18898920 | tf_op jit(solution)/shard_map/while
  222.1 13.8 tile.37
  235.9 4.6 slice-done.2
  240.5 6.5 copy.84
  247.1 6.7 slice.79
  253.7 48.6 %rev.34 = f32[3,512,1024]{2,1,0:T(8,128)} reverse(f32[3,512,1024]{2,1,0:T(8,128)} %slice.79), dimensions={1} | reverse | bytes 12582912 | tf_op jit(solution)/shard_map/while/body/eval_jaxpr/jit(_flip)/rev | solution.py:22
  302.4 4.6 fusion.139
  329.6 52.6 %reduce-scatter.9.cloned.1.call-done = f32[512,384]{1,0:T(8,128)} async-done(((f32[2048,384]{1,0:T(8,128)}), f32[512,384]{1,0:T(8,128)}) %reduce-scatter.9.cloned.1.call-update) | async-done | bytes 786448 | tf_op jit(solution)/shard_map/reduce_scatter | solution.py:172
  397.4 13.7 all-to-all-done
  418.1 5.4 fusion.72
  423.6 10.0 multiply_reduce_fusion.3
  433.6 9.4 fusion.34
  443.0 4.6 fusion.95
  455.4 12.5 all-to-all-done.3
  470.7 30.1 %all-gather.6.cloned.1.call-done = bf16[2048,384]{1,0:T(8,128)(2,1)} async-done(((bf16[512,384]{1,0:T(8,128)(2,1)}), bf16[2048,384]{1,0:T(8,128)(2,1)}) %all-gather.6.cloned.1.call-update) | async-done | bytes 1572880 | tf_op jit(solution)/shard_map/all_gather | solution.py:245
  504.3 9.1 reduce-scatter.11.cloned.1.call-done
  516.0 495.5 %while.38 = (s32[]{:T(128)}, f32[1024,3,64]{0,2,1:T(8,128)}, f32[1024,3,64]{0,2,1:T(8,128)}, f32[3,2047]{1,0:T(4,128)}, bf16[2,512,3,64]{1,3,2,0:T(8,128)(2,1)},...) while((s32[]{:T(128)}, f32[1024,3,64]{0,2,1:T(8,128)}, ...), condition=%wide.region_22.23_spmd.clone, body=%wide.region_19.22_spmd.clone.sunk | while | flops 1030751744 | bytes 378812896 | solution.py:101
  525.6 4.9 tile.38
  530.6 15.2 %reshape.416 = f32[2362365]{0:T(1024)} reshape(f32[3,513,1535]{2,1,0:T(8,128)} %tile.38) | data formatting | bytes 18898920 | tf_op jit(solution)/shard_map/while
  545.7 14.0 tile.39
  564.3 6.5 copy.85
  570.9 6.7 slice.81
  577.5 48.5 %rev.35 = f32[3,512,1024]{2,1,0:T(8,128)} reverse(f32[3,512,1024]{2,1,0:T(8,128)} %slice.81), dimensions={1} | reverse | bytes 12582912 | tf_op jit(solution)/shard_map/while/body/eval_jaxpr/jit(_flip)/rev | solution.py:22
  626.1 8.0 multiply_reduce_fusion.7
  637.7 6.0 fusion.151
  646.2 48.4 %rev.36 = f32[3,512,1024]{2,1,0:T(8,128)} reverse(f32[3,512,1024]{2,1,0:T(8,128)} %copy-done.1), dimensions={1} | reverse | bytes 12582912 | tf_op jit(solution)/shard_map/while/body/eval_jaxpr/transpose(jvp(jit(_flip)))/rev | solution.py:22
  698.6 19.9 %copy.86 = f32[1,3,512,1536]{3,1,2,0:T(4,128)S(1)} copy(f32[1,3,512,1536]{3,2,1,0:T(8,128)S(1)} %pad_bitcast_fusion.2) | data formatting | bytes 18874368 | tf_op jit(solution)/shard_map/while
  718.5 5.2 pad.33
  723.6 14.2 reshape.417
  737.8 16.5 %reshape.418 = f32[3,513,1535]{2,1,0:T(8,128)} reshape(f32[2362365]{0:T(1024)} %reshape.417) | data formatting | bytes 18898920 | tf_op jit(solution)/shard_map/while/body/eval_jaxpr/transpose(jvp())/reshape | solution.py:20
  769.2 4.9 tile.38
  774.1 15.2 %reshape.416 = f32[2362365]{0:T(1024)} reshape(f32[3,513,1535]{2,1,0:T(8,128)} %tile.38) | data formatting | bytes 18898920 | tf_op jit(solution)/shard_map/while
  789.3 14.2 tile.39
  808.1 6.5 copy.85
  814.7 6.7 slice.81
  821.3 48.5 %rev.35 = f32[3,512,1024]{2,1,0:T(8,128)} reverse(f32[3,512,1024]{2,1,0:T(8,128)} %slice.81), dimensions={1} | reverse | bytes 12582912 | tf_op jit(solution)/shard_map/while/body/eval_jaxpr/jit(_flip)/rev | solution.py:22
  869.9 8.0 multiply_reduce_fusion.7
  881.5 6.0 fusion.151
  889.9 48.4 %rev.36 = f32[3,512,1024]{2,1,0:T(8,128)} reverse(f32[3,512,1024]{2,1,0:T(8,128)} %copy-done.1), dimensions={1} | reverse | bytes 12582912 | tf_op jit(solution)/shard_map/while/body/eval_jaxpr/transpose(jvp(jit(_flip)))/rev | solution.py:22
  942.4 19.9 %copy.86 = f32[1,3,512,1536]{3,1,2,0:T(4,128)S(1)} copy(f32[1,3,512,1536]{3,2,1,0:T(8,128)S(1)} %pad_bitcast_fusion.2) | data formatting | bytes 18874368 | tf_op jit(solution)/shard_map/while
  962.2 5.1 pad.33
  967.4 14.2 reshape.417
  981.6 16.3 %reshape.418 = f32[3,513,1535]{2,1,0:T(8,128)} reshape(f32[2362365]{0:T(1024)} %reshape.417) | data formatting | bytes 18898920 | tf_op jit(solution)/shard_map/while/body/eval_jaxpr/transpose(jvp())/reshape | solution.py:20
  1018.5 9.6 all-gather.8.cloned.1.call-done
  1032.5 4.7 bitcast_convert_fusion
  1037.3 10.3 convolution_convert_fusion
  1049.0 8.2 convolution_convert_fusion.1
  1065.8 11.5 all-to-all-done.1
  1084.2 22.4 %reduce-scatter.13.cloned.1.call-done = bf16[512,384]{1,0:T(8,128)(2,1)} async-done(((bf16[2048,384]{1,0:T(8,128)(2,1)}), bf16[512,384]{1,0:T(8,128)(2,1)}) %reduce-scatter.13.cloned.1.call-update) | async-done | bytes 393232 | tf_op jit(solution)/shard_map/reduce_scatter | solution.py:265
  1108.4 45.0 %all-reduce.2 = (f32[12,32]{1,0:T(8,128)}, f32[768]{0:T(1024)}, f32[768]{0:T(1024)}, f32[768,16]{0,1:T(8,128)}) all-reduce(f32[12,32]{1,0:T(8,128)S(1)} %dynamic_update_slice.44, f32[768]{0:T(1024)S(1)} %dynamic_update_slice.45, f32[768]{0:T(1024)S(1)} %copy-done.59, ...), channel_id=1, replica_groups=mesh['dp'=4,'row'=4,'col'=2] {'dp','row','col'}, use_global_device_ids=true, to_apply=%region_28.29 | all-reduce | flops 14208 | bytes 113664 | tf_op jit(solution)/shard_map/psum | solution.py:292
  1158.9 112.4 %reduce-scatter.17.cloned.1.call-done = bf16[2,768,768]{2,1,0:T(8,128)(2,1)} async-done(((bf16[2,3072,768]{2,1,0:T(8,128)(2,1)}), bf16[2,768,768]{2,1,0:T(8,128)(2,1)}) %reduce-scatter.17.cloned.1.call-update) | async-done | bytes 2359312 | tf_op jit(solution)/shard_map/reduce_scatter | solution.py:299
  1275.5 160.2 %reduce-scatter.15.cloned.1.call-done = bf16[2,768,768]{2,1,0:T(8,128)(2,1)} async-done(((bf16[2,3072,768]{2,1,0:T(8,128)(2,1)}), bf16[2,768,768]{2,1,0:T(8,128)(2,1)}) %reduce-scatter.15.cloned.1.call-update) | async-done | bytes 2359312 | tf_op jit(solution)/shard_map/reduce_scatter | solution.py:296
  (354 shorter events, 180.7 us)
Async XLA Ops:
  7.2 38.8 %copy-start = (bf16[3,384,192]{1,2,0:T(8,128)(2,1)S(1)}, bf16[3,384,192]{1,2,0:T(8,128)(2,1)}, u32[]{:S(2)}) copy-start(bf16[3,384,192]{1,2,0:T(8,128)(2,1)} %param.18) | copy-start | bytes 1327108
  7.2 38.8 %all-gather.4.cloned.1.call-start = ((), (), s32[]{:S(2)}) async-start(), calls=%async_computation.10 | async-start | bytes 1966080 | tf_op jit(solution)/shard_map/all_gather | solution.py:151
  9.9 41.1 %copy-start.17 = (f32[512,768]{1,0:T(8,128)}, f32[512,768]{1,0:T(8,128)S(1)}, u32[]{:S(2)}) copy-start(f32[512,768]{1,0:T(8,128)S(1)} %convert_element_type.138) | copy-start | bytes 4718596
  10.6 40.4 %copy-start.52 = (f32[512]{0:T(512)}, f32[512]{0:T(512)S(1)}, u32[]{:S(2)}) copy-start(f32[512]{0:T(512)S(1)} %get-tuple-element.607) | copy-start | bytes 6148
  12.2 51.6 %reduce-scatter.7.cloned.1.call-start = ((), (), s32[]{:S(2)}) async-start(), calls=%async_computation.11 | async-start | bytes 7077888 | tf_op jit(solution)/shard_map/reduce_scatter | solution.py:153
  51.0 331.2 %reduce-scatter.9.cloned.1.call-start = ((), (), s32[]{:S(2)}) async-start(), calls=%async_computation.12 | async-start | bytes 3932160 | tf_op jit(solution)/shard_map/reduce_scatter | solution.py:172
  53.1 14.4 copy-start.36
  139.0 48.6 %copy-start.2 = (bf16[1024,3,64]{0,2,1:T(8,128)(2,1)S(1)}, bf16[1024,3,64]{0,2,1:T(8,128)(2,1)}, u32[]{:S(2)}) copy-start(bf16[1024,3,64]{0,2,1:T(8,128)(2,1)} %get-tuple-element.804) | copy-start | bytes 1179652 | tf_op jit(solution)/shard_map/while
  139.0 48.6 %copy-start.7 = (pred[512,1024]{1,0:T(8,128)(4,1)S(1)}, pred[512,1024]{1,0:T(8,128)(4,1)}, u32[]{:S(2)}) copy-start(pred[512,1024]{1,0:T(8,128)(4,1)} %broadcast_compare_fusion.4) | copy-start | bytes 1572868 | tf_op jit(solution)/shard_map/while
  139.0 48.6 %copy-start.8 = (bf16[1024,3,64]{0,2,1:T(8,128)(2,1)S(1)}, bf16[1024,3,64]{0,2,1:T(8,128)(2,1)}, u32[]{:S(2)}) copy-start(bf16[1024,3,64]{0,2,1:T(8,128)(2,1)} %get-tuple-element.803) | copy-start | bytes 1179652 | tf_op jit(solution)/shard_map/while
  253.7 48.6 %copy-start.2 = (bf16[1024,3,64]{0,2,1:T(8,128)(2,1)S(1)}, bf16[1024,3,64]{0,2,1:T(8,128)(2,1)}, u32[]{:S(2)}) copy-start(bf16[1024,3,64]{0,2,1:T(8,128)(2,1)} %get-tuple-element.804) | copy-start | bytes 1179652 | tf_op jit(solution)/shard_map/while
  253.7 48.6 %copy-start.7 = (pred[512,1024]{1,0:T(8,128)(4,1)S(1)}, pred[512,1024]{1,0:T(8,128)(4,1)}, u32[]{:S(2)}) copy-start(pred[512,1024]{1,0:T(8,128)(4,1)} %broadcast_compare_fusion.4) | copy-start | bytes 1572868 | tf_op jit(solution)/shard_map/while
  253.7 48.6 %copy-start.8 = (bf16[1024,3,64]{0,2,1:T(8,128)(2,1)S(1)}, bf16[1024,3,64]{0,2,1:T(8,128)(2,1)}, u32[]{:S(2)}) copy-start(bf16[1024,3,64]{0,2,1:T(8,128)(2,1)} %get-tuple-element.803) | copy-start | bytes 1179652 | tf_op jit(solution)/shard_map/while
  320.2 62.1 %copy-start.18 = (f32[512,768]{1,0:T(8,128)S(1)}, f32[512,768]{1,0:T(8,128)}, u32[]{:S(2)}) copy-start(f32[512,768]{1,0:T(8,128)} %copy-done.17) | copy-start | bytes 4718596
  325.3 61.1 %all-to-all-start.2 = ((f32[8,2,64,384]{3,2,1,0:T(8,128)}), f32[8,2,64,384]{3,2,1,0:T(8,128)}, u32[]{:S(2)}, u32[]{:S(2)}) async-start(f32[8,2,64,384]{3,2,1,0:T(8,128)} %bitcast.203), calls=%async_computation.4 | async-start | bytes 3145728 | tf_op jit(solution)/shard_map/all_to_all | solution.py:191
  386.4 24.7 %all-to-all-start = ((f32[8,2,64,384]{3,2,1,0:T(8,128)}), f32[8,2,64,384]{3,2,1,0:T(8,128)S(1)}, u32[]{:S(2)}, u32[]{:S(2)}) async-start(f32[8,2,64,384]{3,2,1,0:T(8,128)} %bitcast.202), calls=%async_computation.2 | async-start | bytes 3145728 | tf_op jit(solution)/shard_map/all_to_all | solution.py:190
  390.2 57.4 %copy-start.62 = (f32[2,16]{1,0:T(2,128)}, f32[2,16]{1,0:T(2,128)S(1)}, u32[]{:S(2)}) copy-start(f32[2,16]{1,0:T(2,128)S(1)} %get-tuple-element.608) | copy-start | bytes 388
  416.2 34.0 %copy-start.4 = (f32[2,256,768]{2,1,0:T(8,128)}, f32[2,256,768]{2,1,0:T(8,128)S(1)}, u32[]{:S(2)}) copy-start(f32[2,256,768]{2,1,0:T(8,128)S(1)} %reshape.346) | copy-start | bytes 4718596
  416.3 33.9 %copy-start.45 = (f32[2,256]{1,0:T(2,128)}, f32[2,256]{1,0:T(2,128)S(1)}, u32[]{:S(2)}) copy-start(f32[2,256]{1,0:T(2,128)S(1)} %rsqrt.27) | copy-start | bytes 6148
  418.0 29.6 %copy-start.41 = (f32[2,256,16]{1,2,0:T(8,128)}, f32[2,256,16]{1,2,0:T(8,128)S(1)}, u32[]{:S(2)}) copy-start(f32[2,256,16]{1,2,0:T(8,128)S(1)} %get-tuple-element.611) | copy-start | bytes 98308
  418.1 29.6 %copy-start.50 = (f32[2,256]{1,0:T(2,128)}, f32[2,256]{1,0:T(2,128)S(1)}, u32[]{:S(2)}) copy-start(f32[2,256]{1,0:T(2,128)S(1)} %get-tuple-element.610) | copy-start | bytes 6148
  423.5 10.2 copy-start.27
  423.6 24.1 %copy-start.56 = (f32[2,256]{1,0:T(2,128)}, f32[2,256]{1,0:T(2,128)S(1)}, u32[]{:S(2)}) copy-start(f32[2,256]{1,0:T(2,128)S(1)} %select_reduce_fusion) | copy-start | bytes 6148
  423.6 19.4 %slice-start.4 = ((s8[9437184]{0:T(1024)(128)(4,1)}), s8[4194304]{0:T(1024)(128)(4,1)S(1)}, s32[]{:S(2)}) async-start(s8[9437184]{0:T(1024)(128)(4,1)} %bitcast.200), calls=%async_computation.24 | async-start | bytes 8388608
  423.6 19.4 %slice-start.5 = ((s8[9437184]{0:T(1024)(128)(4,1)}), s8[4194304]{0:T(1024)(128)(4,1)S(1)}, s32[]{:S(2)}) async-start(s8[9437184]{0:T(1024)(128)(4,1)} %bitcast.200), calls=%async_computation.25 | async-start | bytes 8388608
  433.6 14.1 copy-start.64
  433.6 9.4 slice-start.6
  451.7 16.1 %all-to-all-start.3 = ((bf16[8,2,64,384]{3,2,1,0:T(8,128)(2,1)}), bf16[8,2,64,384]{3,2,1,0:T(8,128)(2,1)S(1)}, u32[]{:S(2)}, u32[]{:S(2)}) async-start(bf16[8,2,64,384]{3,2,1,0:T(8,128)(2,1)} %bitcast.30), calls=%async_computation.5 | async-start | bytes 1572864 | tf_op jit(solution)/shard_map/all_to_all | solution.py:234
  455.3 45.5 %all-gather.6.cloned.1.call-start = ((), (), s32[]{:S(2)}) async-start(), calls=%async_computation.13 | async-start | bytes 1966080 | tf_op jit(solution)/shard_map/all_gather | solution.py:245
  455.4 14.3 copy-start.60
  468.0 32.8 %copy-start.40 = (bf16[192,384]{1,0:T(8,128)(2,1)S(1)}, bf16[192,384]{1,0:T(8,128)(2,1)}, u32[]{:S(2)}) copy-start(bf16[192,384]{1,0:T(8,128)(2,1)} %param.19) | copy-start | bytes 442372
  469.6 34.5 %copy-start.25 = (f32[512,384]{1,0:T(8,128)}, f32[512,384]{1,0:T(8,128)S(1)}, u32[]{:S(2)}) copy-start(f32[512,384]{1,0:T(8,128)S(1)} %gather_fusion.1) | copy-start | bytes 2359300
  470.6 45.4 %copy-start.21 = (bf16[1024,3,64]{0,2,1:T(8,128)(2,1)S(1)}, bf16[1024,3,64]{0,2,1:T(8,128)(2,1)}, u32[]{:S(2)}) copy-start(bf16[1024,3,64]{0,2,1:T(8,128)(2,1)} %get-tuple-element.892) | copy-start | bytes 1179652
  470.6 42.8 %reduce-scatter.11.cloned.1.call-start = ((), (), s32[]{:S(2)}) async-start(), calls=%async_computation.14 | async-start | bytes 2359296 | tf_op jit(solution)/shard_map/reduce_scatter | solution.py:248
  504.2 523.9 %all-gather.8.cloned.1.call-start = ((), (), s32[]{:S(2)}) async-start(), calls=%async_computation.15 | async-start | bytes 3538944 | tf_op jit(solution)/shard_map/all_gather | solution.py:262
  516.4 9.3 copy-start.15
  577.5 48.6 %copy-start.3 = (bf16[1024,3,64]{0,2,1:T(8,128)(2,1)S(1)}, bf16[1024,3,64]{0,2,1:T(8,128)(2,1)}, u32[]{:S(2)}) copy-start(bf16[1024,3,64]{0,2,1:T(8,128)(2,1)} %get-tuple-element.861) | copy-start | bytes 1179652 | tf_op jit(solution)/shard_map/while
  577.5 48.6 %copy-start.6 = (pred[512,1024]{1,0:T(8,128)(4,1)S(1)}, pred[512,1024]{1,0:T(8,128)(4,1)}, u32[]{:S(2)}) copy-start(pred[512,1024]{1,0:T(8,128)(4,1)} %broadcast_compare_fusion.5) | copy-start | bytes 1572868 | tf_op jit(solution)/shard_map/while
  577.5 56.6 %slice-start = ((s8[6291456]{0:T(1024)(128)(4,1)}), s8[2097152]{0:T(1024)(128)(4,1)S(1)}, s32[]{:S(2)}) async-start(s8[6291456]{0:T(1024)(128)(4,1)} %bitcast.189), calls=%async_computation.20 | async-start | bytes 4194304 | tf_op jit(solution)/shard_map/while
  626.1 8.1 slice-start.1
  646.1 48.4 %copy-start.14 = (f32[1024,3,64]{0,2,1:T(8,128)}, f32[1024,3,64]{0,2,1:T(8,128)S(1)}, u32[]{:S(2)}) copy-start(f32[1024,3,64]{0,2,1:T(8,128)S(1)} %fusion.150) | copy-start | bytes 2359300 | tf_op jit(solution)/shard_map/while
  760.0 9.3 copy-start.15
  821.3 48.6 %copy-start.3 = (bf16[1024,3,64]{0,2,1:T(8,128)(2,1)S(1)}, bf16[1024,3,64]{0,2,1:T(8,128)(2,1)}, u32[]{:S(2)}) copy-start(bf16[1024,3,64]{0,2,1:T(8,128)(2,1)} %get-tuple-element.861) | copy-start | bytes 1179652 | tf_op jit(solution)/shard_map/while
  821.3 48.6 %copy-start.6 = (pred[512,1024]{1,0:T(8,128)(4,1)S(1)}, pred[512,1024]{1,0:T(8,128)(4,1)}, u32[]{:S(2)}) copy-start(pred[512,1024]{1,0:T(8,128)(4,1)} %broadcast_compare_fusion.5) | copy-start | bytes 1572868 | tf_op jit(solution)/shard_map/while
  821.3 56.6 %slice-start = ((s8[6291456]{0:T(1024)(128)(4,1)}), s8[2097152]{0:T(1024)(128)(4,1)S(1)}, s32[]{:S(2)}) async-start(s8[6291456]{0:T(1024)(128)(4,1)} %bitcast.189), calls=%async_computation.20 | async-start | bytes 4194304 | tf_op jit(solution)/shard_map/while
  869.9 8.0 slice-start.1
  889.9 48.4 %copy-start.14 = (f32[1024,3,64]{0,2,1:T(8,128)}, f32[1024,3,64]{0,2,1:T(8,128)S(1)}, u32[]{:S(2)}) copy-start(f32[1024,3,64]{0,2,1:T(8,128)S(1)} %fusion.150) | copy-start | bytes 2359300 | tf_op jit(solution)/shard_map/while
  1015.8 64.7 %all-reduce.6.cloned.1.call-start = ((), (), s32[]{:S(2)}) async-start(), calls=%async_computation.19 | async-start | bytes 1179648 | tf_op jit(solution)/shard_map/psum | solution.py:283
  1032.4 74.2 %reduce-scatter.13.cloned.1.call-start = ((), (), s32[]{:S(2)}) async-start(), calls=%async_computation.16 | async-start | bytes 1966080 | tf_op jit(solution)/shard_map/reduce_scatter | solution.py:265
  1037.2 234.1 %reduce-scatter.17.cloned.1.call-start = ((), (), s32[]{:S(2)}) async-start(), calls=%async_computation.18 | async-start | bytes 11796480 | tf_op jit(solution)/shard_map/reduce_scatter | solution.py:299
  1047.6 388.1 %reduce-scatter.15.cloned.1.call-start = ((), (), s32[]{:S(2)}) async-start(), calls=%async_computation.17 | async-start | bytes 11796480 | tf_op jit(solution)/shard_map/reduce_scatter | solution.py:296
  1057.2 7.4 copy-start.42
  1057.3 7.4 copy-start.51
  1057.3 7.4 copy-start.63
  1057.3 7.4 copy-start.65
  1060.6 16.8 %copy-start.61 = (s32[1024]{0:T(1024)S(1)}, s32[1024]{0:T(1024)}, u32[]{:S(2)}) copy-start(s32[1024]{0:T(1024)} %copy-done.60) | copy-start | bytes 12292
  1060.6 16.6 %all-to-all-start.1 = ((bf16[8,2,64,384]{3,2,1,0:T(8,128)(2,1)}), bf16[8,2,64,384]{3,2,1,0:T(8,128)(2,1)S(1)}, u32[]{:S(2)}, u32[]{:S(2)}) async-start(bf16[8,2,64,384]{3,2,1,0:T(8,128)(2,1)} %bitcast.24), calls=%async_computation.3 | async-start | bytes 1572864 | tf_op jit(solution)/shard_map/all_to_all | solution.py:225
  1077.5 29.2 %copy-start.53 = (f32[512]{0:T(512)S(1)}, f32[512]{0:T(512)}, u32[]{:S(2)}) copy-start(f32[512]{0:T(512)} %copy-done.52) | copy-start | bytes 6148
  1077.5 29.2 %copy-start.55 = (f32[384]{0:T(512)S(1)}, f32[384]{0:T(512)}, u32[]{:S(2)}) copy-start(f32[384]{0:T(512)} %copy-done.54) | copy-start | bytes 4612
  1079.8 28.7 %copy-start.59 = (f32[768]{0:T(1024)S(1)}, f32[768]{0:T(1024)}, u32[]{:S(2)}) copy-start(f32[768]{0:T(1024)} %get-tuple-element.537) | copy-start | bytes 9220
  1079.8 76.2 %copy-start.19 = (f32[512,768]{1,0:T(8,128)S(1)}, f32[512,768]{1,0:T(8,128)}, u32[]{:S(2)}) copy-start(f32[512,768]{1,0:T(8,128)} %copy-done.17) | copy-start | bytes 4718596
  1079.8 76.2 %copy-start.26 = (f32[512,384]{1,0:T(8,128)S(1)}, f32[512,384]{1,0:T(8,128)}, u32[]{:S(2)}) copy-start(f32[512,384]{1,0:T(8,128)} %copy-done.25) | copy-start | bytes 2359300
  1079.8 76.2 %copy-start.29 = (bf16[512,384]{1,0:T(8,128)(2,1)S(1)}, bf16[512,384]{1,0:T(8,128)(2,1)}, u32[]{:S(2)}) copy-start(bf16[512,384]{1,0:T(8,128)(2,1)} %param.29) | copy-start | bytes 1179652
  1079.8 76.2 %copy-start.66 = (f32[512]{0:T(512)S(1)}, f32[512]{0:T(512)}, u32[]{:S(2)}) copy-start(f32[512]{0:T(512)} %get-tuple-element.606) | copy-start | bytes 6148
  (54 other events, 159.2 us)
Sparse Core Ops, SparseCore 0:
  12.3 33.6 all-gather.3
  51.2 12.5 reduce-scatter.6
  320.3 61.9 reduce-scatter.8
  470.7 30.0 all-gather.5
  504.3 9.0 reduce-scatter.10
  1016.0 12.1 all-gather.7
  1032.5 40.7 all-reduce.5
  1076.3 30.2 reduce-scatter.12
  1109.0 162.2 reduce-scatter.16
  1273.5 162.1 reduce-scatter.14
where the time goes:
time: 1470 us; the launch traced here: 1450 us
  local copies, waits for them, and re-layouts  659 us (45%)
  waiting for transfers between devices  479 us (33%)
  matrix products  130 us (9%)
  other arithmetic  61 us (4%)
  blocking collectives  49.8 us (3%)
  loops' own time  36.3 us (2%)
  starting transfers between devices  16.1 us (1%)
  between operations  15.2 us (1%)
    rev x6, local copies, waits for them, and re-layouts, skewed_bias(): return jnp.flip(shifted, axis=1)  291 us
    while x114, local copies, waits for them, and re-layouts  168 us
    reduce_scatter x1, waiting for transfers between devices, shards(): lax.psum_scatter(d_up.astype(jnp.bfloat16), 'dp', scatter_dimension=1, ti...  160 us
    reduce_scatter x1, waiting for transfers between devices, shards(): lax.psum_scatter(d_down.astype(jnp.bfloat16), 'dp', scatter_dimension=1,...  112 us
    another operation x8, local copies, waits for them, and re-layouts, skewed_bias(): jnp.tile(table_seg, (1, block_rows + 1))[:, :block_rows * (seg_len + 1)]  75.6 us
    reduce_scatter x1, waiting for transfers between devices, shards(): lax.psum_scatter(jnp.dot(part_rows, w_proj, preferred_element_type=jnp.fl...  52.6 us
    psum x1, blocking collectives, shards(): lax.psum((gain_whole, d_gain_ffn, d_router, rel_whole), ('dp', 'row', 'co...  45 us
    all_gather x1, waiting for transfers between devices, shards(): gathered = lax.all_gather(normed_half, 'row', axis=0, tiled=True)  33.8 us
  transfers between devices with their start and end apart: 14, of which 12 were waited for; matrix products, arithmetic and copies ran while one was open for 4% of the time, Pallas kernels for 0%

commit v1 on v0

v1 whole, which is shorter than its diff:
```python
from functools import partial

import jax
import jax.numpy as jnp
from jax import lax
from jax.experimental import pallas as pl
from jax.experimental.pallas import tpu as pltpu
from jax.sharding import PartitionSpec as P

H = 12
HD = 64
NB = 32
EXP_DEV = 2
SUB = 128

epsilon = 1e-06
highest = lax.Precision.HIGHEST
f32 = jnp.float32
bf16 = jnp.bfloat16
group = ("row", "col")

NT = (((1,), (1,)), ((), ()))
NN = (((1,), (0,)), ((), ()))
TN = (((0,), (0,)), ((), ()))


def mm(a, b, dims=NN):
    return lax.dot_general(a, b, dims, preferred_element_type=f32)


def fill_strip(table_ref, strip_ref):
    heads, _, span = strip_ref.shape
    for h in range(heads):
        rows = jnp.broadcast_to(table_ref[h : h + 1, :], (SUB, table_ref.shape[1]))
        rolled = pltpu.roll(rows, table_ref.shape[1] - (SUB - 1), 1, stride=1, stride_axis=0)
        strip_ref[h] = rolled[:, :span]


def strip_at(step, part, parts, length):
    begin = length - SUB * (step * parts + part + 1)
    return pl.ds(pl.multiple_of(begin, SUB), length)


def forward_kernel(
    qkv_ref, table_ref, seg_col_ref, seg_row_ref, out_ref, lse_ref, strip_ref, *, rows, heads
):
    step = pl.program_id(0)
    length = qkv_ref.shape[0]
    inner = heads * HD

    @pl.when(step == 0)
    def _():
        fill_strip(table_ref, strip_ref)

    here = pl.ds(pl.multiple_of(step * rows, rows), rows)
    same = seg_col_ref[here, :] == seg_row_ref[...]
    q_all = qkv_ref[here, :inner] * jnp.asarray(HD**-0.5, bf16)
    lane = lax.broadcasted_iota(jnp.int32, lse_ref.shape, 1)
    lse = jnp.zeros(lse_ref.shape, f32)
    outs = []
    parts = rows // SUB
    for h in range(heads):
        lo = h * HD
        keys = qkv_ref[:, inner + lo : inner + lo + HD]
        values = qkv_ref[:, 2 * inner + lo : 2 * inner + lo + HD]
        scores = mm(q_all[:, lo : lo + HD], keys, NT)
        bias = jnp.concatenate(
            [strip_ref[h, :, strip_at(step, u, parts, length)] for u in range(parts)], axis=0
        )
        scores = jnp.where(same, scores + bias, -1e9)
        top = jnp.max(scores, axis=1, keepdims=True)
        weights = jnp.exp(scores - top)
        total = jnp.sum(weights, axis=1, keepdims=True)
        outs.append(mm(weights.astype(bf16), values) / total)
        lse = jnp.where(lane == h, top + jnp.log(total), lse)
    out_ref[...] = jnp.concatenate(outs, axis=1).astype(bf16)
    lse_ref[...] = lse


def whole(shape):
    return pl.BlockSpec(shape, lambda *_: (0,) * len(shape))


def attend_forward(qkv, table, segments, heads):
    length = qkv.shape[0]
    rows = min(256, length)
    inner = heads * HD
    return pl.pallas_call(
        partial(forward_kernel, rows=rows, heads=heads),
        grid=(length // rows,),
        in_specs=[
            whole(qkv.shape),
            whole(table.shape),
            whole((length, 1)),
            whole((1, length)),
        ],
        out_specs=[
            pl.BlockSpec((rows, inner), lambda i: (i, 0)),
            pl.BlockSpec((rows, SUB), lambda i: (i, 0)),
        ],
        out_shape=[
            jax.ShapeDtypeStruct((length, inner), bf16),
            jax.ShapeDtypeStruct((length, SUB), f32),
        ],
        scratch_shapes=[pltpu.VMEM((heads, SUB, 2 * length - SUB), f32)],
        compiler_params=pltpu.CompilerParams(vmem_limit_bytes=40 * 1024 * 1024),
        cost_estimate=pl.CostEstimate(
            flops=4 * length * length * inner,
            bytes_accessed=10 * length * inner,
            transcendentals=length * length * heads,
        ),
        name="attend_forward",
    )(qkv, table, segments[:, None], segments[None, :])


def backward_kernel(
    qkv_ref,
    grad_ref,
    lse_ref,
    table_ref,
    seg_col_ref,
    seg_row_ref,
    out_ref,
    d_table_ref,
    strip_ref,
    d_strip_ref,
    d_keys_ref,
    d_values_ref,
    *,
    rows,
    heads,
):
    step = pl.program_id(0)
    length = qkv_ref.shape[0]
    inner = heads * HD

    @pl.when(step == 0)
    def _():
        fill_strip(table_ref, strip_ref)
        d_strip_ref[...] = jnp.zeros_like(d_strip_ref)
        d_keys_ref[...] = jnp.zeros_like(d_keys_ref)
        d_values_ref[...] = jnp.zeros_like(d_values_ref)

    here = pl.ds(pl.multiple_of(step * rows, rows), rows)
    same = seg_col_ref[here, :] == seg_row_ref[...]
    q_all = qkv_ref[here, :inner] * jnp.asarray(HD**-0.5, bf16)
    parts = rows // SUB
    d_queries = []
    for h in range(heads):
        lo = h * HD
        keys = qkv_ref[:, inner + lo : inner + lo + HD]
        values = qkv_ref[:, 2 * inner + lo : 2 * inner + lo + HD]
        grads = grad_ref[here, lo : lo + HD]
        queries = q_all[:, lo : lo + HD]
        bias = jnp.concatenate(
            [strip_ref[h, :, strip_at(step, u, parts, length)] for u in range(parts)], axis=0
        )
        scores = mm(queries, keys, NT) + bias - lse_ref[:, h : h + 1]
        probs = jnp.where(same, jnp.exp(jnp.where(same, scores, 0.0)), 0.0)
        d_values_ref[lo : lo + HD, :] += mm(grads, probs.astype(bf16), TN)
        d_probs = mm(grads, values, NT)
        pulled = probs * d_probs
        d_scores = pulled - probs * jnp.sum(pulled, axis=1, keepdims=True)
        for u in range(parts):
            at = strip_at(step, u, parts, length)
            d_strip_ref[h, :, at] += d_scores[u * SUB : (u + 1) * SUB]
        d_raw = d_scores.astype(bf16)
        d_queries.append(mm(d_raw, keys) * HD**-0.5)
        d_keys_ref[lo : lo + HD, :] += mm(queries, d_raw, TN)
    out_ref[here, :inner] = jnp.concatenate(d_queries, axis=1).astype(bf16)

    @pl.when(step == pl.num_programs(0) - 1)
    def _():
        for h in range(heads):
            lo = h * HD
            out_ref[:, inner + lo : inner + lo + HD] = d_keys_ref[lo : lo + HD, :].T.astype(bf16)
            out_ref[:, 2 * inner + lo : 2 * inner + lo + HD] = d_values_ref[
                lo : lo + HD, :
            ].T.astype(bf16)
            summed = jnp.concatenate([d_strip_ref[h], jnp.zeros((SUB, SUB), f32)], axis=1)
            count = SUB
            while count > 1:
                count //= 2
                summed = summed[count:] + pltpu.roll(summed[:count], count, 1)
            d_table_ref[h : h + 1, :] = summed


def attend_backward(qkv, d_head, lse, table, segments, heads):
    length = qkv.shape[0]
    rows = min(256, length)
    inner = heads * HD
    return pl.pallas_call(
        partial(backward_kernel, rows=rows, heads=heads),
        grid=(length // rows,),
        in_specs=[
            whole(qkv.shape),
            whole(d_head.shape),
            pl.BlockSpec((rows, SUB), lambda i: (i, 0)),
            whole(table.shape),
            whole((length, 1)),
            whole((1, length)),
        ],
        out_specs=[whole(qkv.shape), whole(table.shape)],
        out_shape=[
            jax.ShapeDtypeStruct(qkv.shape, bf16),
            jax.ShapeDtypeStruct(table.shape, f32),
        ],
        scratch_shapes=[
            pltpu.VMEM((heads, SUB, 2 * length - SUB), f32),
            pltpu.VMEM((heads, SUB, 2 * length - SUB), f32),
            pltpu.VMEM((inner, length), f32),
            pltpu.VMEM((inner, length), f32),
        ],
        compiler_params=pltpu.CompilerParams(vmem_limit_bytes=48 * 1024 * 1024),
        cost_estimate=pl.CostEstimate(
            flops=10 * length * length * inner,
            bytes_accessed=16 * length * inner,
            transcendentals=length * length * heads,
        ),
        name="attend_backward",
    )(qkv, d_head, lse, table, segments[:, None], segments[None, :])


def joined(block_ref, first):
    rows, cols = block_ref.shape[0], block_ref.shape[1]
    slots, half = block_ref.shape[3], block_ref.shape[4] // 2
    lo = 0 if first else half
    return jnp.concatenate(
        [
            block_ref[:, c, 0, :, lo : lo + half].reshape(rows * slots, half)
            for c in range(cols)
        ],
        axis=1,
    )


GELU_A = 0.7978845608028654
GELU_B = 0.044715


def gelu_pair(u):
    square = u * u
    bent = jnp.tanh(GELU_A * u * (1.0 + GELU_B * square))
    value = 0.5 * u * (1.0 + bent)
    slope = 0.5 * (1.0 + bent) + (0.5 * GELU_A) * u * (1.0 - bent * bent) * (
        1.0 + 3.0 * GELU_B * square
    )
    return value, slope


def expert_kernel(got_ref, up_ref, down_ref, back_ref, x_ref, g_ref, out_ref, grad_ref):
    step = pl.program_id(1)

    @pl.when(step == 0)
    def _():
        x_ref[...] = joined(got_ref, True)
        g_ref[...] = joined(got_ref, False)

    up, down = up_ref[0], down_ref[0]
    value, slope = gelu_pair(mm(x_ref[...], up, NT))
    out = mm(value.astype(bf16), down)
    d_pre = (mm(g_ref[...], down, NT) * slope).astype(bf16)
    grad = mm(d_pre, up)

    @pl.when(step == 0)
    def _():
        out_ref[...] = out
        grad_ref[...] = grad

    @pl.when(step > 0)
    def _():
        out_ref[...] += out
        grad_ref[...] += grad

    @pl.when(step == pl.num_programs(1) - 1)
    def _():
        rows, cols, _, slots, both = back_ref.shape
        half = both // 2
        for c in range(cols):
            for lo, source in ((0, out_ref), (half, grad_ref)):
                back_ref[:, c, 0, :, lo : lo + half] = (
                    source[:, c * half : (c + 1) * half].astype(bf16).reshape(rows, slots, half)
                )


def run_experts(got, w_up, w_down):
    rows, cols, experts, slots, both = got.shape
    hidden, width = w_up.shape[1:]
    tile = 512
    block = pl.BlockSpec((rows, cols, 1, slots, both), lambda e, f: (0, 0, e, 0, 0))
    weight = pl.BlockSpec((1, tile, width), lambda e, f: (e, f, 0))
    tokens = rows * slots
    return pl.pallas_call(
        expert_kernel,
        grid=(experts, hidden // tile),
        in_specs=[block, weight, weight],
        out_specs=block,
        out_shape=jax.ShapeDtypeStruct(got.shape, bf16),
        scratch_shapes=[
            pltpu.VMEM((tokens, width), bf16),
            pltpu.VMEM((tokens, width), bf16),
            pltpu.VMEM((tokens, width), f32),
            pltpu.VMEM((tokens, width), f32),
        ],
        compiler_params=pltpu.CompilerParams(vmem_limit_bytes=40 * 1024 * 1024),
        cost_estimate=pl.CostEstimate(
            flops=8 * experts * tokens * hidden * width,
            bytes_accessed=4 * experts * hidden * width,
            transcendentals=experts * tokens * hidden,
        ),
        name="experts",
    )(got, w_up, w_down)


def weight_kernel(at_ref, got_ref, up_ref, down_ref, d_up_ref, d_down_ref):
    step = pl.program_id(1)
    block = got_ref.at[0]
    x, g = joined(block, True), joined(block, False)
    value, slope = gelu_pair(mm(up_ref[0], x, NT))
    d_pre = (mm(down_ref[0], g, NT) * slope).astype(bf16)
    d_down = mm(value.astype(bf16), g)
    d_up = mm(d_pre, x)

    @pl.when(step == 0)
    def _():
        d_up_ref[0] = d_up
        d_down_ref[0] = d_down

    @pl.when(step > 0)
    def _():
        d_up_ref[0] += d_up
        d_down_ref[0] += d_down


def weight_grads(got_all, w_up, w_down, dp_at):
    parts, rows, cols, experts, slots, both = got_all.shape
    hidden, width = w_up.shape[1:]
    own = hidden // parts
    weight = pl.BlockSpec((1, own, width), lambda e, n, at: (e, at[0], 0))
    result = pl.BlockSpec((1, own, width), lambda e, n, at: (e, 0, 0))
    shape = jax.ShapeDtypeStruct((experts, own, width), f32)
    return pl.pallas_call(
        weight_kernel,
        grid_spec=pltpu.PrefetchScalarGridSpec(
            num_scalar_prefetch=1,
            grid=(experts, parts),
            in_specs=[
                pl.BlockSpec(
                    (1, rows, cols, 1, slots, both), lambda e, n, at: (n, 0, 0, e, 0, 0)
                ),
                weight,
                weight,
            ],
            out_specs=[result, result],
        ),
        out_shape=[shape, shape],
        compiler_params=pltpu.CompilerParams(vmem_limit_bytes=40 * 1024 * 1024),
        cost_estimate=pl.CostEstimate(
            flops=8 * experts * parts * rows * slots * own * width,
            bytes_accessed=12 * experts * own * width + 2 * got_all.size,
            transcendentals=experts * parts * rows * slots * own,
        ),
        name="weight_grads",
    )(dp_at[None], got_all, w_up, w_down)


def pairs_out(k):
    return [
        (r * 2 + c, ((2 * (r % 2) + c) ^ k) * 2 + r // 2) for r in range(4) for c in range(2)
    ]


def pairs_home(k):
    return [(b, a) for a, b in pairs_out(k)]


def swap_col(array):
    return lax.ppermute(array, "col", [(0, 1), (1, 0)])


def total_over(array, axis):
    count = lax.axis_size(axis)
    stride = 1
    while stride < count:
        array = array + lax.ppermute(array, axis, [(i, i ^ stride) for i in range(count)])
        stride *= 2
    return array


def shards(
    layer_in,
    w_qkv,
    w_proj,
    rel_bias,
    rel_bucket,
    segment_ids,
    gain_attn,
    gain_ffn,
    w_router,
    routes,
    w_up,
    w_down,
    d_layer,
):
    row_count = lax.axis_size("row")
    col_count = lax.axis_size("col")
    dp_at = lax.axis_index("dp")
    row_at = lax.axis_index("row")
    col_at = lax.axis_index("col")
    tok_dev, width = layer_in.shape
    slot_count = max(2, tok_dev // 8)
    half_width = width // col_count
    quarter = tok_dev // 2
    length = segment_ids.shape[1]
    inner = w_qkv.shape[2]
    heads_dev = inner // HD
    experts_all = EXP_DEV * row_count * col_count
    home = 2 * (row_at % 2) + col_at
    is_first = col_at == 0

    def both_halves(mine, other, axis):
        return jnp.where(
            is_first,
            jnp.concatenate([mine, other], axis),
            jnp.concatenate([other, mine], axis),
        )

    def my_half(array, axis):
        size = array.shape[axis] // 2
        return lax.dynamic_slice_in_dim(array, col_at * size, size, axis)

    def other_half(array, axis):
        size = array.shape[axis] // 2
        return lax.dynamic_slice_in_dim(array, (1 - col_at) * size, size, axis)

    def in_order(chunks, at):
        stacked = jnp.stack(chunks)
        return jnp.concatenate(
            [lax.dynamic_index_in_dim(stacked, i ^ at, 0, False) for i in range(len(chunks))], 0
        )

    own_tokens = my_half(layer_in, 0)
    tokens_seq = in_order(
        [lax.ppermute(own_tokens, group, pairs_out(k)) for k in range(row_count)], row_at
    ).astype(f32)
    w_pair = both_halves(w_qkv, swap_col(w_qkv), 1)
    w_all = jnp.concatenate([w_pair[0], w_pair[1], w_pair[2]], axis=1)
    scale_seq = lax.rsqrt(jnp.mean(tokens_seq * tokens_seq, axis=-1, keepdims=True) + epsilon)
    normed = (tokens_seq * scale_seq * gain_attn).astype(bf16)
    qkv = mm(normed, w_all).astype(bf16)

    buckets = (rel_bucket[:, None] == jnp.arange(NB, dtype=jnp.int32)[None, :]).astype(f32)
    bias_rows = lax.dynamic_slice_in_dim(rel_bias, row_at * heads_dev, heads_dev, 0)
    bias_table = jnp.einsum("hb,ob->ho", bias_rows, buckets, precision=highest)
    table = jnp.pad(bias_table, ((0, 0), (0, 1)))
    segments = segment_ids[0]

    w_proj_late, qkv = lax.optimization_barrier((w_proj, qkv))
    proj_half = lax.all_gather(w_proj_late, "row", axis=0, tiled=False)
    proj_half = jnp.stack(
        [
            lax.dynamic_index_in_dim(proj_half, home ^ k, 0, False)
            for k in range(row_count)
        ]
    )
    proj_swapped = swap_col(proj_half)
    proj_other = jnp.stack([proj_swapped[k ^ 1] for k in range(row_count)])
    proj_all = both_halves(proj_half, proj_other, 2).reshape(row_count * inner, width)
    grads_in = both_halves(d_layer, swap_col(d_layer), 1).astype(f32)

    head_out, lse = attend_forward(qkv, table, segments, heads_dev)

    head_blocks = head_out.reshape(2, tok_dev, inner)
    heads = jnp.concatenate(
        [
            lax.ppermute(
                lax.dynamic_index_in_dim(head_blocks, (row_at ^ k) // 2, 0, False),
                group,
                pairs_home(k),
            )
            for k in range(row_count)
        ],
        axis=1,
    )
    middle = layer_in.astype(f32) + mm(heads, proj_all)
    scale_ffn = lax.rsqrt(jnp.mean(middle * middle, axis=-1, keepdims=True) + epsilon)
    hidden = middle * scale_ffn * gain_ffn
    gate_probs = jax.nn.softmax(jnp.dot(hidden, w_router, precision=highest), axis=-1)
    routed = routes[:, 0]
    chosen = routed[:, None] == jnp.arange(experts_all, dtype=jnp.int32)[None, :]
    gating = jnp.sum(jnp.where(chosen, gate_probs, 0.0), axis=-1, keepdims=True)
    counts = jnp.cumsum(chosen.astype(jnp.int32), axis=0)
    slot_index = jnp.sum(jnp.where(chosen, counts, 0), axis=-1) - 1
    placed = routed * slot_count + slot_index
    slots_all = experts_all * slot_count
    placing = (jnp.arange(slots_all, dtype=jnp.int32)[:, None] == placed[None, :]).astype(bf16)

    payload = jnp.concatenate(
        [
            my_half(hidden, 1).astype(bf16),
            (gating * d_layer.astype(f32)).astype(bf16),
        ],
        axis=1,
    )
    send = mm(placing, payload).astype(bf16)
    send = send.reshape(row_count * col_count, EXP_DEV, slot_count, width)
    got = lax.all_to_all(send, group, split_axis=0, concat_axis=0, tiled=True)
    got_all = lax.all_gather(got, "dp", axis=0, tiled=False)
    block_shape = (row_count, col_count, EXP_DEV, slot_count, width)
    back = run_experts(got.reshape(block_shape), w_up, w_down)
    back = lax.all_to_all(
        back.reshape(send.shape), group, split_axis=0, concat_axis=0, tiled=True
    )
    mine = mm(placing, back.reshape(slots_all, width), TN).astype(bf16)
    other = swap_col(mine)
    expert_out = both_halves(mine[:, :half_width], other[:, :half_width], 1).astype(f32)
    d_hidden = both_halves(mine[:, half_width:], other[:, half_width:], 1).astype(f32)

    layer_out = my_half(middle, 1) + gating * mine[:, :half_width].astype(f32)
    d_gating = jnp.sum(grads_in * expert_out, axis=-1, keepdims=True)
    d_logits = d_gating * gate_probs * (chosen.astype(f32) - gating)
    d_hidden = d_hidden + jnp.einsum("tn,dn->td", d_logits, w_router, precision=highest)
    d_router = 0.5 * jnp.einsum("tn,td->nd", d_logits, hidden, precision=highest)
    d_gain_ffn = 0.5 * jnp.sum(middle * scale_ffn * d_hidden, axis=0)
    scaled_ffn = d_hidden * gain_ffn
    d_middle = (
        grads_in
        + scale_ffn * scaled_ffn
        - middle * scale_ffn**3 * jnp.mean(scaled_ffn * middle, axis=-1, keepdims=True)
    )
    d_attn = d_middle.astype(bf16)
    d_heads = mm(my_half(d_attn, 0), proj_all, NT).astype(bf16)
    d_head = in_order(
        [
            lax.ppermute(d_heads[:, k * inner : (k + 1) * inner], group, pairs_out(k))
            for k in range(row_count)
        ],
        row_at,
    )
    d_proj = mm(heads, my_half(d_attn, 1), TN).astype(bf16).reshape(row_count, inner, half_width)
    d_proj = in_order([d_proj[k] for k in range(row_count)], home)
    d_proj = lax.psum_scatter(d_proj, "row", scatter_dimension=0, tiled=True)
    d_proj = lax.psum(d_proj, "dp").astype(f32)

    d_qkv, d_table = attend_backward(qkv, d_head, lse, table, segments, heads_dev)

    part_normed = mm(d_qkv, w_all, NT).astype(bf16).reshape(row_count, quarter, width)
    d_normed = sum(
        lax.ppermute(
            lax.dynamic_index_in_dim(part_normed, row_at ^ k, 0, False), group, pairs_home(k)
        ).astype(f32)
        for k in range(row_count)
    )

    d_w = mm(normed, d_qkv, TN)
    gain_part = jnp.sum(d_w * w_all.astype(f32), axis=1) / gain_attn
    d_w = my_half(d_w, 0) + swap_col(other_half(d_w, 0).astype(bf16)).astype(f32)
    d_w = lax.psum(d_w.astype(bf16), "dp").astype(f32)
    d_w_qkv = d_w.reshape(half_width, 3, inner).transpose(1, 0, 2)

    d_rel_part = jnp.einsum("ho,ob->hb", d_table[:, : 2 * length - 1], buckets, precision=highest)
    rel_whole = lax.dynamic_update_slice_in_dim(
        jnp.zeros((H, NB), f32), d_rel_part, row_at * heads_dev, 0
    )
    rel_row = jnp.pad(rel_whole.reshape(1, H * NB), ((0, 0), (0, width - H * NB)))
    small = jnp.concatenate([d_router, d_gain_ffn[None], gain_part[None], rel_row], axis=0)
    small = total_over(total_over(total_over(small, "col"), "row"), "dp")
    d_w_router = small[:experts_all].T
    d_gain_ffn = small[experts_all]
    d_gain_attn = small[experts_all + 1]
    d_rel_bias = small[experts_all + 2, : H * NB].reshape(H, NB)

    own = own_tokens.astype(f32)
    scale_own = lax.rsqrt(jnp.mean(own * own, axis=-1, keepdims=True) + epsilon)
    scaled_attn = d_normed * gain_attn
    d_own = (
        my_half(d_middle, 0)
        + scale_own * scaled_attn
        - own * scale_own**3 * jnp.mean(scaled_attn * own, axis=-1, keepdims=True)
    )
    d_layer_in = both_halves(my_half(d_own, 1), swap_col(other_half(d_own, 1)), 0)

    d_up, d_down = weight_grads(
        got_all.reshape((got_all.shape[0],) + block_shape), w_up, w_down, dp_at
    )
    return (
        layer_out,
        d_layer_in,
        d_w_qkv,
        d_proj,
        d_rel_bias,
        d_gain_attn,
        d_gain_ffn,
        d_w_router,
        d_up,
        d_down,
    )


def solution(mesh):
    placed = (
        P(("dp", "row"), None),
        P(None, "col", "row"),
        P("row", "col"),
        P(),
        P(),
        P(("dp", "col"), None),
        P(),
        P(),
        P(),
        P(("dp", "row"), None),
        P(("row", "col"), None, None),
        P(("row", "col"), None, None),
        P(("dp", "row"), "col"),
    )
    return jax.shard_map(
        shards,
        mesh=mesh,
        in_specs=placed,
        out_specs=(
            P(("dp", "row"), "col"),
            P(("dp", "row"), "col"),
            P(None, "col", "row"),
            P("row", "col"),
            P(),
            P(),
            P(),
            P(),
            P(("row", "col"), "dp", None),
            P(("row", "col"), "dp", None),
        ),
        check_vma=False,
    )
```

time: 1470 us -> 398 us (0.27); the launches traced: 1450 us -> 396 us
  local copies, waits for them, and re-layouts: 659 us -> 18.5 us
  waiting for transfers between devices: 479 us -> 151 us
  matrix products: 130 us -> 21.1 us
  Pallas kernels: 0 us -> 69.5 us
  other arithmetic: 61 us -> 23.7 us
  loops' own time: 36.3 us -> 0 us
  starting transfers between devices: 16.1 us -> 37.8 us
    reduce_scatter x6 -> x1, waiting for transfers between devices: 367 us -> 0.01 us  [shards(): d_proj = lax.psum_scatter(d_proj, 'row', scatter_dimension=0, tiled=True)]
    rev x6 -> x0, local copies, waits for them, and re-layouts: 291 us -> none  [skewed_bias(): return jnp.flip(shifted, axis=1)]
    while x114 -> x0, local copies, waits for them, and re-layouts: 168 us -> none
    dot_general x29 -> x12, matrix products: 124 us -> 19.1 us  [the longest x8 13.7 us: mm(): return lax.dot_general(a, b, dims, preferred_element_type=f32)]
    another operation x13 -> x3, local copies, waits for them, and re-layouts: 78.9 us -> 0.9 us  [the longest x1 0.68 us: shards(): d_rel_bias = small[experts_all + 2, :H * NB].reshape(H, NB)]
    pallas_call x0 -> x4, Pallas kernels: none -> 69.5 us  [the longest x1 21.9 us: weight_grads(): pl.pallas_call(weight_kernel, grid_spec=pltpu.PrefetchScalarGridSpec(num_...]
    ppermute x0 -> x27, waiting for transfers between devices: none -> 48.1 us  [the longest x5 25.5 us: total_over(): lax.ppermute(array, axis, [(i, i ^ stride) for i in range(count)])]
    psum x2 -> x0, blocking collectives: 47.5 us -> none  [the longest x1 45 us: shards(): lax.psum((gain_whole, d_gain_ffn, d_router, rel_whole), ('dp', 'row', 'co...]
  transfers between devices with their start and end apart: 14 -> 30, of which waited for: 12 -> 12; matrix products, arithmetic and copies ran while one was open for 4% -> 8% of each run, Pallas kernels for 0% -> 7%
where the time goes in v1:
time: 398 us; the launch traced here: 396 us
  waiting for transfers between devices  151 us (38%)
  Pallas kernels  69.5 us (17%)
  blocking collectives  59.5 us (15%)
  starting transfers between devices  37.8 us (9%)
  other arithmetic  23.7 us (6%)
  matrix products  21.1 us (5%)
  local copies, waits for them, and re-layouts  18.5 us (5%)
  between operations  15 us (4%)
    all_gather x1, waiting for transfers between devices, shards(): got_all = lax.all_gather(got, 'dp', axis=0, tiled=False)  102 us
    ppermute x5, waiting for transfers between devices, total_over(): lax.ppermute(array, axis, [(i, i ^ stride) for i in range(count)])  25.5 us
    all_to_all x1, blocking collectives, shards(): got = lax.all_to_all(send, group, split_axis=0, concat_axis=0, tiled=True)  24 us
    all_to_all x1, blocking collectives, shards(): lax.all_to_all(back.reshape(send.shape), group, split_axis=0, concat_axis...  23.4 us
    pallas_call x1, Pallas kernels, weight_grads(): pl.pallas_call(weight_kernel, grid_spec=pltpu.PrefetchScalarGridSpec(num_...  21.9 us
    pallas_call x1, Pallas kernels, run_experts(): pl.pallas_call(expert_kernel, grid=(experts, hidden // tile), in_specs=[b...  19.4 us
    pallas_call x1, Pallas kernels, attend_backward(): pl.pallas_call(partial(backward_kernel, rows=rows, heads=heads), grid=(le...  19.2 us
    dot_general x8, matrix products, mm(): return lax.dot_general(a, b, dims, preferred_element_type=f32)  13.7 us
  transfers between devices with their start and end apart: 30, of which 12 were waited for; matrix products, arithmetic and copies ran while one was open for 8% of the time, Pallas kernels for 7%

profile of v1, /device:TPU:0, one launch (start us, length us, event | category | flops | bytes accessed | tf_op | source)
XLA Modules:
  0.0 396.2 jit_solution(13232374509513208882)
XLA Ops:
  7.2 1.0 constant_dynamic-slice_fusion.7
  8.3 5.8 %collective-permute-start.3 = (bf16[256,768]{1,0:T(8,128)(2,1)S(1)}, bf16[256,768]{1,0:T(8,128)(2,1)S(1)}, u32[]{:S(2)}, u32[]{:S(2)}) collective-permute-start(bf16[256,768]{1,0:T(8,128)(2,1)S(1)} %constant_dynamic-slice_fusion.7), channel_id=1, source_target_pairs={{0,6},{1,4},{2,2},{3,0},{4,7},{5,5},{6,3},{7,1},{8,14},{9,12},{10,... | collective-permute-start | bytes 1179656 | tf_op jit(solution)/shard_map/ppermute | solution.py:444
  14.2 2.0 collective-permute-start.1
  16.9 1.7 collective-permute-start.4
  19.2 1.1 reduce-window.6
  20.4 2.1 fusion.12
  22.4 1.1 collective-permute-done.3
  23.5 7.0 %collective-permute-done.2 = bf16[256,768]{1,0:T(8,128)(2,1)S(1)} collective-permute-done((bf16[256,768]{1,0:T(8,128)(2,1)S(1)}, bf16[256,768]{1,0:T(8,128)(2,1)S(1)}, u32[]{:S(2)}, u32[]{:S(2)}) %collective-permute-start.2) | collective-permute-done | bytes 393248 | tf_op jit(solution)/shard_map/ppermute | solution.py:444
  30.5 1.1 collective-permute-done.1
  32.4 0.9 copy-done.26
  33.6 1.5 convolution_convert_fusion.1.qkv_ref
  35.2 12.1 %all-gather = bf16[768,384]{1,0:T(8,128)(2,1)S(1)} all-gather(bf16[192,384]{1,0:T(8,128)(2,1)S(1)} %copy-done.34), channel_id=2, replica_groups=mesh['dp'=4,'row'=4,'col'=2] {'row'}, dimensions={0}, use_global_device_ids=true | all-gather | bytes 737280 | tf_op jit(solution)/shard_map/all_gather | solution.py:459
  47.3 0.9 pad_maximum_fusion.4
  49.0 8.9 %attend_forward.1 = (bf16[1024,192]{1,0:T(8,128)(2,1)S(1)}, f32[1024,128]{1,0:T(8,128)S(1)}) custom-call(bf16[1024,576]{1,0:T(8,128)(2,1)S(1)} %convolution_convert_fusion.1.qkv_ref, f32[3,2048]{1,0:T(4,128)S(1)} %pad.8.table_ref, s32[1024,1]{1,0:T(8,128)S(1)} %copy.30.seg_col_ref, s32[1,1024]{1,0:T(1,128)S(1)} %copy-done.3), custom_call_target="tpu_custom_call" | custom-call | flops 805306368 | bytes 1966080 | tf_op jit(solution)/shard_map/attend_forward/pallas_call | solution.py:88
  58.0 3.3 collective-permute-start.8
  61.4 1.8 collective-permute-start.6
  63.9 1.2 fusion.53
  65.2 5.0 %collective-permute-done.8 = bf16[512,192]{1,0:T(8,128)(2,1)S(1)} collective-permute-done((bf16[512,192]{1,0:T(8,128)(2,1)S(1)}, bf16[512,192]{1,0:T(8,128)(2,1)S(1)}, u32[]{:S(2)}, u32[]{:S(2)}) %collective-permute-start.8) | collective-permute-done | bytes 196640 | tf_op jit(solution)/shard_map/ppermute | solution.py:476
  70.1 4.8 %collective-permute-done.7 = bf16[512,192]{1,0:T(8,128)(2,1)S(1)} collective-permute-done((bf16[512,192]{1,0:T(8,128)(2,1)S(1)}, bf16[512,192]{1,0:T(8,128)(2,1)S(1)}, u32[]{:S(2)}, u32[]{:S(2)}) %collective-permute-start.7) | collective-permute-done | bytes 196640 | tf_op jit(solution)/shard_map/ppermute | solution.py:476
  75.0 2.6 multiply_reduce_fusion.3
  78.8 1.4 fusion.55
  80.4 1.1 multiply_convert_fusion
  81.6 1.0 fusion.5
  82.6 24.0 %all_to_all.10 = bf16[8,2,64,768]{3,2,1,0:T(8,128)(2,1)S(1)} all-to-all(bf16[8,2,64,768]{3,2,1,0:T(8,128)(2,1)S(1)} %bitcast.110), channel_id=1, replica_groups=mesh['dp'=4,'row'=4,'col'=2] {'row','col'}, dimensions={0} | all-to-all | bytes 3145728 | tf_op jit(solution)/shard_map/all_to_all | solution.py:507
  106.6 4.2 %copy-done.4 = bf16[2,3072,768]{2,1,0:T(8,128)(2,1)S(1)} copy-done((bf16[2,3072,768]{2,1,0:T(8,128)(2,1)S(1)}, bf16[2,3072,768]{2,1,0:T(8,128)(2,1)}, u32[]{:S(2)}) %copy-start.4) | copy-done | bytes 9437208
  110.9 19.4 %experts.1 = bf16[4,2,2,64,768]{4,3,2,1,0:T(8,128)(2,1)S(1)} custom-call(bf16[4,2,2,64,768]{4,3,2,1,0:T(8,128)(2,1)S(1)} %bitcast.103, bf16[2,3072,768]{2,1,0:T(8,128)(2,1)S(1)} %copy-done.4, bf16[2,3072,768]{2,1,0:T(8,128)(2,1)} %down_ref.3), custom_call_target="tpu_custom_call" | custom-call | flops 9663676416 | bytes 18874368 | tf_op jit(solution)/shard_map/experts/pallas_call | solution.py:293
  130.3 23.4 %all_to_all.11 = bf16[8,2,64,768]{3,2,1,0:T(8,128)(2,1)S(1)} all-to-all(bf16[8,2,64,768]{3,2,1,0:T(8,128)(2,1)S(1)} %bitcast.105), channel_id=1, replica_groups=mesh['dp'=4,'row'=4,'col'=2] {'row','col'}, dimensions={0} | all-to-all | bytes 3145728 | tf_op jit(solution)/shard_map/all_to_all | solution.py:511
  153.7 2.1 fusion.8
  156.3 1.2 fusion.51
  157.6 0.9 collective-permute-done.11
  158.5 1.2 fusion.52
  159.7 1.8 fusion.6
  161.5 2.5 multiply_reduce_fusion.1
  164.0 3.1 fusion.49
  167.1 1.8 convolution_convert_fusion.3
  169.1 2.5 collective-permute-start.15
  171.9 1.7 collective-permute-start.13
  174.4 0.9 convolution_convert_fusion.2
  175.6 0.9 pad_maximum_fusion.7
  176.7 1.3 collective-permute-done.14
  179.1 19.2 %attend_backward.1 = (bf16[1024,576]{1,0:T(8,128)(2,1)S(1)}, f32[3,2048]{1,0:T(4,128)S(1)}) custom-call(bf16[1024,576]{1,0:T(8,128)(2,1)S(1)} %convolution_convert_fusion.1.qkv_ref, bf16[1024,192]{1,0:T(8,128)(2,1)S(1)} %pad_maximum_fusion.9.grad_ref, f32[1024,128]{1,0:T(8,128)S(1)} %copy-done.7, f32[3,2048]{1,0:T(4,128)S(1)} %pad.8.table_ref, ...), custom_call_target="tpu_custom_call" | custom-call | flops 2013265920 | bytes 3145728 | tf_op jit(solution)/shard_map/attend_backward/pallas_call | solution.py:192
  198.5 1.3 multiply_reduce_fusion
  199.9 2.1 collective-permute-start.21
  201.9 1.4 collective-permute-done.21
  207.2 2.4 convolution_convert_fusion
  209.7 1.3 collective-permute-start.23
  211.0 1.2 dynamic-slice_bitcast_fusion.3
  212.2 2.3 collective-permute-start.19
  214.8 2.5 collective-permute-start.17
  217.3 4.5 %collective-permute-start.16 = (bf16[256,768]{1,0:T(8,128)(2,1)}, bf16[256,768]{1,0:T(8,128)(2,1)}, u32[]{:S(2)}, u32[]{:S(2)}) collective-permute-start(bf16[256,768]{1,0:T(8,128)(2,1)} %get-tuple-element.36), channel_id=1, source_target_pairs={{0,0},{2,1},{4,2},{6,3},{1,4},{3,5},{5,6},{7,7},{8,8},{10,9},{12,1... | collective-permute-start | bytes 1179656 | tf_op jit(solution)/shard_map/ppermute | solution.py:549
  221.9 14.2 %collective-permute-done.24 = f32[19,768]{1,0:T(8,128)S(1)} collective-permute-done((f32[19,768]{1,0:T(8,128)S(1)}, f32[19,768]{1,0:T(8,128)S(1)}, u32[]{:S(2)}, u32[]{:S(2)}) %collective-permute-start.24) | collective-permute-done | bytes 58400 | tf_op jit(solution)/shard_map/ppermute | solution.py:385
  236.7 1.5 collective-permute-start.25
  238.2 7.3 %collective-permute-done.25 = f32[19,768]{1,0:T(8,128)} collective-permute-done((f32[19,768]{1,0:T(8,128)}, f32[19,768]{1,0:T(8,128)}, u32[]{:S(2)}, u32[]{:S(2)}) %collective-permute-start.25) | collective-permute-done | bytes 58400 | tf_op jit(solution)/shard_map/ppermute | solution.py:385
  245.5 0.9 add.223
  247.1 2.0 multiply_add_fusion
  249.2 4.0 %collective-permute-done.26 = f32[19,768]{1,0:T(8,128)S(1)} collective-permute-done((f32[19,768]{1,0:T(8,128)S(1)}, f32[19,768]{1,0:T(8,128)S(1)}, u32[]{:S(2)}, u32[]{:S(2)}) %collective-permute-start.26) | collective-permute-done | bytes 58400 | tf_op jit(solution)/shard_map/ppermute | solution.py:385
  253.3 1.4 fusion.13
  254.7 1.4 fusion.15
  258.2 0.9 maximum_select_fusion.5
  259.1 2.0 transpose.39
  261.1 1.7 convert_element_type.123
  262.8 102.3 %all-gather.4.cloned.1.call-done = bf16[32,2,64,768]{3,2,1,0:T(8,128)(2,1)} async-done(((bf16[8,2,64,768]{3,2,1,0:T(8,128)(2,1)}), bf16[32,2,64,768]{3,2,1,0:T(8,128)(2,1)}) %all-gather.4.cloned.1.call-update) | async-done | bytes 6291472 | tf_op jit(solution)/shard_map/all_gather | solution.py:508
  365.1 2.8 copy-done.5
  367.8 21.9 %weight_grads.1 = (f32[2,768,768]{2,1,0:T(8,128)}, f32[2,768,768]{2,1,0:T(8,128)}) custom-call(s32[1]{0:T(128)} %bitcast.51.at_ref, bf16[4,4,2,2,64,768]{5,4,3,2,1,0:T(8,128)(2,1)S(1)} %bitcast.107, bf16[2,3072,768]{2,1,0:T(8,128)(2,1)} %up_ref.3, bf16[2,3072,768]{2,1,0:T(8,128)(2,1)} %down_ref.3), custom_call_target="tpu_custom_call" | custom-call | flops 9663676416 | bytes 20447232 | tf_op jit(solution)/shard_map/weight_grads/pallas_call | solution.py:342
  (199 shorter events, 16.3 us)
Async XLA Ops:
  7.2 71.6 %copy-start = (f32[768,16]{0,1:T(8,128)S(1)}, f32[768,16]{0,1:T(8,128)}, u32[]{:S(2)}) copy-start(f32[768,16]{0,1:T(8,128)} %param.21) | copy-start | bytes 147460
  7.2 197.0 %reduce-scatter.2.cloned.1.call-start = ((), (), s32[]{:S(2)}) async-start(), calls=%async_computation.3 | async-start | bytes 737280 | tf_op jit(solution)/shard_map/reduce_scatter | solution.py:542
  8.3 15.3 %collective-permute-start.3 = (bf16[256,768]{1,0:T(8,128)(2,1)S(1)}, bf16[256,768]{1,0:T(8,128)(2,1)S(1)}, u32[]{:S(2)}, u32[]{:S(2)}) collective-permute-start(bf16[256,768]{1,0:T(8,128)(2,1)S(1)} %constant_dynamic-slice_fusion.7), channel_id=1, source_target_pairs={{0,6},{1,4},{2,2},{3,0},{4,7},{5,5},{6,3},{7,1},{8,14},{9,12},{10,... | collective-permute-start | bytes 1179656 | tf_op jit(solution)/shard_map/ppermute | solution.py:444
  14.1 16.4 %collective-permute-start.2 = (bf16[256,768]{1,0:T(8,128)(2,1)S(1)}, bf16[256,768]{1,0:T(8,128)(2,1)S(1)}, u32[]{:S(2)}, u32[]{:S(2)}) collective-permute-start(bf16[256,768]{1,0:T(8,128)(2,1)S(1)} %constant_dynamic-slice_fusion.7), channel_id=1, source_target_pairs={{0,4},{1,6},{2,0},{3,2},{4,5},{5,7},{6,1},{7,3},{8,12},{9,14},{10,... | collective-permute-start | bytes 1179656 | tf_op jit(solution)/shard_map/ppermute | solution.py:444
  14.2 17.4 %collective-permute-start.1 = (bf16[256,768]{1,0:T(8,128)(2,1)S(1)}, bf16[256,768]{1,0:T(8,128)(2,1)S(1)}, u32[]{:S(2)}, u32[]{:S(2)}) collective-permute-start(bf16[256,768]{1,0:T(8,128)(2,1)S(1)} %constant_dynamic-slice_fusion.7), channel_id=1, source_target_pairs={{0,2},{1,0},{2,6},{3,4},{4,3},{5,1},{6,7},{7,5},{8,10},{9,8},{10,1... | collective-permute-start | bytes 1179656 | tf_op jit(solution)/shard_map/ppermute | solution.py:444
  16.2 15.4 %collective-permute-start = (bf16[256,768]{1,0:T(8,128)(2,1)S(1)}, bf16[256,768]{1,0:T(8,128)(2,1)S(1)}, u32[]{:S(2)}, u32[]{:S(2)}) collective-permute-start(bf16[256,768]{1,0:T(8,128)(2,1)S(1)} %constant_dynamic-slice_fusion.7), channel_id=1, source_target_pairs={{0,0},{1,2},{2,4},{3,6},{4,1},{5,3},{6,5},{7,7},{8,8},{9,10},{10,1... | collective-permute-start | bytes 1179656 | tf_op jit(solution)/shard_map/ppermute | solution.py:444
  16.9 15.5 %collective-permute-start.4 = (bf16[3,384,192]{1,2,0:T(8,128)(2,1)}, bf16[3,384,192]{1,2,0:T(8,128)(2,1)S(1)}, u32[]{:S(2)}, u32[]{:S(2)}) collective-permute-start(bf16[3,384,192]{1,2,0:T(8,128)(2,1)} %param.14), channel_id=1, source_target_pairs={{0,1},{1,0},{2,3},{3,2},{4,5},{5,4},{6,7},{7,6},{8,9},{9,8},{10,11... | collective-permute-start | bytes 1327112 | tf_op jit(solution)/shard_map/ppermute | solution.py:378
  35.1 13.4 %copy-start.3 = (s32[1,1024]{1,0:T(1,128)S(1)}, s32[1,1024]{1,0:T(1,128)}, u32[]{:S(2)}) copy-start(s32[1,1024]{1,0:T(1,128)} %seg_row_ref.3) | copy-start | bytes 12292
  48.2 15.6 %collective-permute-start.9 = (bf16[4,192,384]{2,1,0:T(8,128)(2,1)}, bf16[4,192,384]{2,1,0:T(8,128)(2,1)}, u32[]{:S(2)}, u32[]{:S(2)}) collective-permute-start(bf16[4,192,384]{2,1,0:T(8,128)(2,1)} %pad_maximum_fusion.4), channel_id=1, source_target_pairs={{0,1},{1,0},{2,3},{3,2},{4,5},{5,4},{6,7},{7,6},{8,9},{9,8},{10,11... | collective-permute-start | bytes 1769480 | tf_op jit(solution)/shard_map/ppermute | solution.py:378
  49.0 32.6 %copy-start.45 = (s32[512]{0:T(512)}, s32[512]{0:T(512)S(1)}, u32[]{:S(2)}) copy-start(s32[512]{0:T(512)S(1)} %add_add_fusion) | copy-start | bytes 6148
  57.9 7.1 %copy-start.6 = (f32[1024,128]{1,0:T(8,128)}, f32[1024,128]{1,0:T(8,128)S(1)}, u32[]{:S(2)}) copy-start(f32[1024,128]{1,0:T(8,128)S(1)} %get-tuple-element.21.lse_ref) | copy-start | bytes 1572868
  58.0 17.0 %copy-start.14 = (bf16[512,768]{1,0:T(8,128)(2,1)S(1)}, bf16[512,768]{1,0:T(8,128)(2,1)}, u32[]{:S(2)}) copy-start(bf16[512,768]{1,0:T(8,128)(2,1)} %param.13) | copy-start | bytes 2359300
  58.0 12.1 %collective-permute-start.8 = (bf16[512,192]{1,0:T(8,128)(2,1)S(1)}, bf16[512,192]{1,0:T(8,128)(2,1)S(1)}, u32[]{:S(2)}, u32[]{:S(2)}) collective-permute-start(bf16[512,192]{1,0:T(8,128)(2,1)S(1)} %get-tuple-element.74), channel_id=1, source_target_pairs={{6,0},{4,1},{2,2},{0,3},{7,4},{5,5},{3,6},{1,7},{14,8},{12,9},{10,... | collective-permute-start | bytes 589832 | tf_op jit(solution)/shard_map/ppermute | solution.py:476
  61.3 13.7 %collective-permute-start.7 = (bf16[512,192]{1,0:T(8,128)(2,1)S(1)}, bf16[512,192]{1,0:T(8,128)(2,1)S(1)}, u32[]{:S(2)}, u32[]{:S(2)}) collective-permute-start(bf16[512,192]{1,0:T(8,128)(2,1)S(1)} %get-tuple-element.75), channel_id=1, source_target_pairs={{4,0},{6,1},{0,2},{2,3},{5,4},{7,5},{1,6},{3,7},{12,8},{14,9},{8,1... | collective-permute-start | bytes 589832 | tf_op jit(solution)/shard_map/ppermute | solution.py:476
  61.4 13.6 %collective-permute-start.6 = (bf16[512,192]{1,0:T(8,128)(2,1)S(1)}, bf16[512,192]{1,0:T(8,128)(2,1)S(1)}, u32[]{:S(2)}, u32[]{:S(2)}) collective-permute-start(bf16[512,192]{1,0:T(8,128)(2,1)S(1)} %get-tuple-element.76), channel_id=1, source_target_pairs={{2,0},{0,1},{6,2},{4,3},{3,4},{1,5},{7,6},{5,7},{10,8},{8,9},{14,1... | collective-permute-start | bytes 589832 | tf_op jit(solution)/shard_map/ppermute | solution.py:476
  63.2 11.8 %collective-permute-start.5 = (bf16[512,192]{1,0:T(8,128)(2,1)S(1)}, bf16[512,192]{1,0:T(8,128)(2,1)S(1)}, u32[]{:S(2)}, u32[]{:S(2)}) collective-permute-start(bf16[512,192]{1,0:T(8,128)(2,1)S(1)} %get-tuple-element.73), channel_id=1, source_target_pairs={{0,0},{2,1},{4,2},{6,3},{1,4},{3,5},{5,6},{7,7},{8,8},{10,9},{12,1... | collective-permute-start | bytes 589832 | tf_op jit(solution)/shard_map/ppermute | solution.py:476
  65.2 12.5 %copy-start.24 = (bf16[4,192,384]{2,1,0:T(8,128)(2,1)}, bf16[4,192,384]{2,1,0:T(8,128)(2,1)S(1)}, u32[]{:S(2)}) copy-start(bf16[4,192,384]{2,1,0:T(8,128)(2,1)S(1)} %pad_maximum_fusion.5) | copy-start | bytes 1769476
  70.1 7.5 %copy-start.47 = (bf16[512,192]{1,0:T(8,128)(2,1)}, bf16[512,192]{1,0:T(8,128)(2,1)S(1)}, u32[]{:S(2)}) copy-start(bf16[512,192]{1,0:T(8,128)(2,1)S(1)} %collective-permute-done.8) | copy-start | bytes 589828
  75.0 3.3 copy-start.38
  106.6 23.7 %copy-start.2 = (bf16[8,2,64,768]{3,2,1,0:T(8,128)(2,1)}, bf16[8,2,64,768]{3,2,1,0:T(8,128)(2,1)S(1)}, u32[]{:S(2)}) copy-start(bf16[8,2,64,768]{3,2,1,0:T(8,128)(2,1)S(1)} %all_to_all.10) | copy-start | bytes 4718596
  106.6 4.2 %copy-start.4 = (bf16[2,3072,768]{2,1,0:T(8,128)(2,1)S(1)}, bf16[2,3072,768]{2,1,0:T(8,128)(2,1)}, u32[]{:S(2)}) copy-start(bf16[2,3072,768]{2,1,0:T(8,128)(2,1)} %up_ref.3) | copy-start | bytes 28311556
  130.3 23.4 %copy-start.46 = (s32[512]{0:T(512)S(1)}, s32[512]{0:T(512)}, u32[]{:S(2)}) copy-start(s32[512]{0:T(512)} %copy-done.45) | copy-start | bytes 6148
  155.8 2.6 collective-permute-start.11
  155.8 3.8 collective-permute-start.10
  157.5 3.9 copy-start.11
  164.0 3.1 copy-start.25
  167.1 7.3 %copy-start.48 = (bf16[512,192]{1,0:T(8,128)(2,1)S(1)}, bf16[512,192]{1,0:T(8,128)(2,1)}, u32[]{:S(2)}) copy-start(bf16[512,192]{1,0:T(8,128)(2,1)} %copy-done.47) | copy-start | bytes 589828
  167.1 7.3 %copy-start.50 = (bf16[512,192]{1,0:T(8,128)(2,1)S(1)}, bf16[512,192]{1,0:T(8,128)(2,1)}, u32[]{:S(2)}) copy-start(bf16[512,192]{1,0:T(8,128)(2,1)} %copy-done.49) | copy-start | bytes 589828
  167.1 7.3 %copy-start.52 = (bf16[512,192]{1,0:T(8,128)(2,1)S(1)}, bf16[512,192]{1,0:T(8,128)(2,1)}, u32[]{:S(2)}) copy-start(bf16[512,192]{1,0:T(8,128)(2,1)} %copy-done.51) | copy-start | bytes 589828
  167.1 7.3 %copy-start.54 = (bf16[512,192]{1,0:T(8,128)(2,1)S(1)}, bf16[512,192]{1,0:T(8,128)(2,1)}, u32[]{:S(2)}) copy-start(bf16[512,192]{1,0:T(8,128)(2,1)} %copy-done.53) | copy-start | bytes 589828
  169.1 7.6 %collective-permute-start.15 = (bf16[256,192]{1,0:T(8,128)(2,1)S(1)}, bf16[256,192]{1,0:T(8,128)(2,1)S(1)}, u32[]{:S(2)}, u32[]{:S(2)}) collective-permute-start(bf16[256,192]{1,0:T(8,128)(2,1)S(1)} %get-tuple-element.78), channel_id=1, source_target_pairs={{0,6},{1,4},{2,2},{3,0},{4,7},{5,5},{6,3},{7,1},{8,14},{9,12},{10,... | collective-permute-start | bytes 294920 | tf_op jit(solution)/shard_map/ppermute | solution.py:535
  171.6 6.5 %collective-permute-start.14 = (bf16[256,192]{1,0:T(8,128)(2,1)S(1)}, bf16[256,192]{1,0:T(8,128)(2,1)S(1)}, u32[]{:S(2)}, u32[]{:S(2)}) collective-permute-start(bf16[256,192]{1,0:T(8,128)(2,1)S(1)} %get-tuple-element.79), channel_id=1, source_target_pairs={{0,4},{1,6},{2,0},{3,2},{4,5},{5,7},{6,1},{7,3},{8,12},{9,14},{10,... | collective-permute-start | bytes 294920 | tf_op jit(solution)/shard_map/ppermute | solution.py:535
  171.9 6.1 %collective-permute-start.13 = (bf16[256,192]{1,0:T(8,128)(2,1)S(1)}, bf16[256,192]{1,0:T(8,128)(2,1)S(1)}, u32[]{:S(2)}, u32[]{:S(2)}) collective-permute-start(bf16[256,192]{1,0:T(8,128)(2,1)S(1)} %get-tuple-element.80), channel_id=1, source_target_pairs={{0,2},{1,0},{2,6},{3,4},{4,3},{5,1},{6,7},{7,5},{8,10},{9,8},{10,1... | collective-permute-start | bytes 294920 | tf_op jit(solution)/shard_map/ppermute | solution.py:535
  173.7 4.4 %collective-permute-start.12 = (bf16[256,192]{1,0:T(8,128)(2,1)S(1)}, bf16[256,192]{1,0:T(8,128)(2,1)S(1)}, u32[]{:S(2)}, u32[]{:S(2)}) collective-permute-start(bf16[256,192]{1,0:T(8,128)(2,1)S(1)} %get-tuple-element.77), channel_id=1, source_target_pairs={{0,0},{1,2},{2,4},{3,6},{4,1},{5,3},{6,5},{7,7},{8,8},{9,10},{10,1... | collective-permute-start | bytes 294920 | tf_op jit(solution)/shard_map/ppermute | solution.py:535
  176.5 82.6 %all-reduce.5.cloned.1.call-start = ((), (), s32[]{:S(2)}) async-start(), calls=%async_computation.5 | async-start | bytes 1179648 | tf_op jit(solution)/shard_map/psum | solution.py:558
  179.1 19.3 %copy-start.17 = (bf16[256,768]{1,0:T(8,128)(2,1)S(1)}, bf16[256,768]{1,0:T(8,128)(2,1)}, u32[]{:S(2)}) copy-start(bf16[256,768]{1,0:T(8,128)(2,1)} %copy-done.16) | copy-start | bytes 1179652
  179.1 19.3 %copy-start.19 = (bf16[256,768]{1,0:T(8,128)(2,1)S(1)}, bf16[256,768]{1,0:T(8,128)(2,1)}, u32[]{:S(2)}) copy-start(bf16[256,768]{1,0:T(8,128)(2,1)} %copy-done.18) | copy-start | bytes 1179652
  179.1 19.3 %copy-start.21 = (bf16[256,768]{1,0:T(8,128)(2,1)S(1)}, bf16[256,768]{1,0:T(8,128)(2,1)}, u32[]{:S(2)}) copy-start(bf16[256,768]{1,0:T(8,128)(2,1)} %copy-done.20) | copy-start | bytes 1179652
  179.1 19.3 %copy-start.23 = (bf16[256,768]{1,0:T(8,128)(2,1)S(1)}, bf16[256,768]{1,0:T(8,128)(2,1)}, u32[]{:S(2)}) copy-start(bf16[256,768]{1,0:T(8,128)(2,1)} %copy-done.22) | copy-start | bytes 1179652
  179.1 19.3 %copy-start.28 = (bf16[768,192]{0,1:T(8,128)(2,1)S(1)}, bf16[768,192]{0,1:T(8,128)(2,1)}, u32[]{:S(2)}) copy-start(bf16[768,192]{0,1:T(8,128)(2,1)} %copy-done.27) | copy-start | bytes 884740
  179.1 19.3 %copy-start.31 = (bf16[768,192]{0,1:T(8,128)(2,1)S(1)}, bf16[768,192]{0,1:T(8,128)(2,1)}, u32[]{:S(2)}) copy-start(bf16[768,192]{0,1:T(8,128)(2,1)} %copy-done.30) | copy-start | bytes 884740
  179.1 19.3 %copy-start.33 = (bf16[768,192]{0,1:T(8,128)(2,1)S(1)}, bf16[768,192]{0,1:T(8,128)(2,1)}, u32[]{:S(2)}) copy-start(bf16[768,192]{0,1:T(8,128)(2,1)} %copy-done.32) | copy-start | bytes 884740
  179.1 19.3 %copy-start.43 = (f32[1024]{0:T(1024)S(1)}, f32[1024]{0:T(1024)}, u32[]{:S(2)}) copy-start(f32[1024]{0:T(1024)} %copy-done.42) | copy-start | bytes 12292
  199.8 5.2 %copy-start.44 = (f32[768]{0:T(1024)S(1)}, f32[768]{0:T(1024)}, u32[]{:S(2)}) copy-start(f32[768]{0:T(1024)} %get-tuple-element.26) | copy-start | bytes 9220
  199.8 5.2 %copy-start.9 = (f32[512,768]{1,0:T(8,128)S(1)}, f32[512,768]{1,0:T(8,128)}, u32[]{:S(2)}) copy-start(f32[512,768]{1,0:T(8,128)} %copy-done.8) | copy-start | bytes 4718596
  199.8 5.2 %copy-start.40 = (f32[512]{0:T(512)S(1)}, f32[512]{0:T(512)}, u32[]{:S(2)}) copy-start(f32[512]{0:T(512)} %copy-done.39) | copy-start | bytes 6148
  199.9 3.5 collective-permute-start.21
  204.3 3.0 copy-start.29
  204.3 160.8 %all-gather.4.cloned.1.call-start = ((), (), s32[]{:S(2)}) async-start(), calls=%async_computation.4 | async-start | bytes 7864320 | tf_op jit(solution)/shard_map/all_gather | solution.py:508
  206.8 2.9 collective-permute-start.22
  209.7 12.1 %collective-permute-start.23 = (f32[19,768]{1,0:T(8,128)S(1)}, f32[19,768]{1,0:T(8,128)S(1)}, u32[]{:S(2)}, u32[]{:S(2)}) collective-permute-start(f32[19,768]{1,0:T(8,128)S(1)} %fusion.48), channel_id=1, source_target_pairs={{0,2},{2,0},{4,6},{6,4},{1,3},{3,1},{5,7},{7,5},{8,10},{10,8},{12,... | collective-permute-start | bytes 175112 | tf_op jit(solution)/shard_map/ppermute | solution.py:385
  211.0 36.2 %copy-start.12 = (f32[512,768]{1,0:T(8,128)S(1)}, f32[512,768]{1,0:T(8,128)}, u32[]{:S(2)}) copy-start(f32[512,768]{1,0:T(8,128)} %copy-done.10) | copy-start | bytes 4718596
  212.2 41.1 %copy-start.15 = (bf16[512,768]{1,0:T(8,128)(2,1)S(1)}, bf16[512,768]{1,0:T(8,128)(2,1)}, u32[]{:S(2)}) copy-start(bf16[512,768]{1,0:T(8,128)(2,1)} %param.13) | copy-start | bytes 2359300
  212.2 41.0 %collective-permute-start.19 = (bf16[256,768]{1,0:T(8,128)(2,1)}, bf16[256,768]{1,0:T(8,128)(2,1)S(1)}, u32[]{:S(2)}, u32[]{:S(2)}) collective-permute-start(bf16[256,768]{1,0:T(8,128)(2,1)} %get-tuple-element.37), channel_id=1, source_target_pairs={{6,0},{4,1},{2,2},{0,3},{7,4},{5,5},{3,6},{1,7},{14,8},{12,9},{10,... | collective-permute-start | bytes 1179656 | tf_op jit(solution)/shard_map/ppermute | solution.py:549
  214.5 38.7 %collective-permute-start.18 = (bf16[256,768]{1,0:T(8,128)(2,1)}, bf16[256,768]{1,0:T(8,128)(2,1)S(1)}, u32[]{:S(2)}, u32[]{:S(2)}) collective-permute-start(bf16[256,768]{1,0:T(8,128)(2,1)} %get-tuple-element.38), channel_id=1, source_target_pairs={{4,0},{6,1},{0,2},{2,3},{5,4},{7,5},{1,6},{3,7},{12,8},{14,9},{8,1... | collective-permute-start | bytes 1179656 | tf_op jit(solution)/shard_map/ppermute | solution.py:549
  214.8 38.4 %collective-permute-start.17 = (bf16[256,768]{1,0:T(8,128)(2,1)}, bf16[256,768]{1,0:T(8,128)(2,1)S(1)}, u32[]{:S(2)}, u32[]{:S(2)}) collective-permute-start(bf16[256,768]{1,0:T(8,128)(2,1)} %get-tuple-element.39), channel_id=1, source_target_pairs={{2,0},{0,1},{6,2},{4,3},{3,4},{1,5},{7,6},{5,7},{10,8},{8,9},{14,1... | collective-permute-start | bytes 1179656 | tf_op jit(solution)/shard_map/ppermute | solution.py:549
  217.3 35.9 %collective-permute-start.16 = (bf16[256,768]{1,0:T(8,128)(2,1)}, bf16[256,768]{1,0:T(8,128)(2,1)}, u32[]{:S(2)}, u32[]{:S(2)}) collective-permute-start(bf16[256,768]{1,0:T(8,128)(2,1)} %get-tuple-element.36), channel_id=1, source_target_pairs={{0,0},{2,1},{4,2},{6,3},{1,4},{3,5},{5,6},{7,7},{8,8},{10,9},{12,1... | collective-permute-start | bytes 1179656 | tf_op jit(solution)/shard_map/ppermute | solution.py:549
  221.8 14.3 %collective-permute-start.24 = (f32[19,768]{1,0:T(8,128)S(1)}, f32[19,768]{1,0:T(8,128)S(1)}, u32[]{:S(2)}, u32[]{:S(2)}) collective-permute-start(f32[19,768]{1,0:T(8,128)S(1)} %add.221), channel_id=1, source_target_pairs={{0,4},{2,6},{4,0},{6,2},{1,5},{3,7},{5,1},{7,3},{8,12},{10,14},{12... | collective-permute-start | bytes 175112 | tf_op jit(solution)/shard_map/ppermute | solution.py:385
  236.7 8.8 %collective-permute-start.25 = (f32[19,768]{1,0:T(8,128)}, f32[19,768]{1,0:T(8,128)}, u32[]{:S(2)}, u32[]{:S(2)}) collective-permute-start(f32[19,768]{1,0:T(8,128)} %add.222), channel_id=1, source_target_pairs={{0,8},{8,0},{16,24},{24,16},{1,9},{9,1},{17,25},{25,17},{2,10},{10... | collective-permute-start | bytes 175112 | tf_op jit(solution)/shard_map/ppermute | solution.py:385
  246.4 6.8 %collective-permute-start.26 = (f32[19,768]{1,0:T(8,128)S(1)}, f32[19,768]{1,0:T(8,128)S(1)}, u32[]{:S(2)}, u32[]{:S(2)}) collective-permute-start(f32[19,768]{1,0:T(8,128)S(1)} %add.223), channel_id=1, source_target_pairs={{0,16},{8,24},{16,0},{24,8},{1,17},{9,25},{17,1},{25,9},{2,18},{10... | collective-permute-start | bytes 175112 | tf_op jit(solution)/shard_map/ppermute | solution.py:385
  249.1 5.5 %copy-start.13 = (f32[512,768]{1,0:T(8,128)S(1)}, f32[512,768]{1,0:T(8,128)}, u32[]{:S(2)}) copy-start(f32[512,768]{1,0:T(8,128)} %get-tuple-element.35) | copy-start | bytes 4718596
  256.2 2.0 collective-permute-start.20
  365.1 2.8 copy-start.5
  367.8 21.9 %copy-start.1 = (f32[768,16]{0,1:T(8,128)S(1)}, f32[768,16]{0,1:T(8,128)}, u32[]{:S(2)}) copy-start(f32[768,16]{0,1:T(8,128)} %param.21) | copy-start | bytes 147460
  (22 other events, 39.7 us)
Sparse Core Ops, SparseCore 0:
  176.6 27.1 reduce-scatter.1
  206.9 40.8 all-reduce.4
  249.5 115.5 all-gather.3
